TPU v7x, 128 devices: a whole 4x4x4 slice. The times are simulated.
128 devices in a mesh: lat: 4 (over y), lon: 32 (over x, z, core).
Axes of the slice: x: 4, y: 4, z: 4, core: 2. Of those that a mesh axis runs over, the one named last changes fastest.
Arguments:
- state: bfloat16 [64, 128, 12288], P(None, 'lat', 'lon'), may hold values from -6 to 6
- forcing: bfloat16 [64, 128, 12288], P(None, 'lat', 'lon'), may hold values from -6 to 6
- conv_weight: bfloat16 [9, 64, 64], replicated, may hold values from -0.25 to 0.25
- w_first: bfloat16 [128, 512], replicated, may hold values from -0.5 to 0.5
- b_first: float32 [512], replicated, may hold values from -3 to 3
- w_second: bfloat16 [512, 512], replicated, may hold values from -0.25 to 0.25
- b_second: float32 [512], replicated, may hold values from -3 to 3
- w_third: bfloat16 [512, 512], replicated, may hold values from -0.25 to 0.25
- b_third: float32 [512], replicated, may hold values from -3 to 3
- w_final: bfloat16 [512, 128], replicated, may hold values from -0.25 to 0.25
- b_final: float32 [128], replicated, may hold values from -3 to 3
- active: int32 [128, 12288], P('lat', 'lon'), may hold values from 0 to 1
- owner: int32 [128, 12288], P('lat', 'lon'), may hold values from 0 to 31, as said below
- slot: int32 [128, 12288], P('lat', 'lon'), may hold values from 0 to 255, as said below
- source: int32 [4, 32, 8192], P('lat', 'lon'), may hold values from 0 to 12288, as said below
Outputs:
- new_state: bfloat16 [64, 128, 12288], P(None, 'lat', 'lon')
- owned: bfloat16 [64, 4, 32, 32, 256], P(None, 'lat', 'lon')
Inputs may be any that keep to these rules, and one draw needn't show every extreme that they name: Only cells with active = 1 are owned; owner names a device of the same lat index. Among the active cells of one device the pairs (owner, slot) are distinct, and the slots used for one owner are 0 up to their count minus one. In every lat index some device hands exactly 256 columns to an owner, and every owner receives exactly 4096 columns from the devices of its lat index together. source[r, s, owner*256+slot] is the cell number of the active cell of tile (r, s) with that owner and slot, and every other entry is 12288.
All inputs are finite; a program needn't handle non-finite values.
Results may differ from a plain program's by a relative error of at most 0.0052.
Values may be sent and summed in bfloat16 or wider, within the bound.
No kernel may reach another device: no remote copies, remote signals or barrier semaphores. Data moves between devices by JAX's collectives and lax.ppermute only.
A program may use at most 128 MiB of HBM per device.

v0:
```python
import jax
import jax.numpy as jnp
from jax import lax
from jax.sharding import PartitionSpec as P

SLOTS_DEV = 8192


def with_halo(block, sides, width, periodic):
    for axis, dim in sides:
        count = lax.axis_size(axis)
        forward = [(i, i + 1) for i in range(count - 1)]
        if periodic:
            forward.append((count - 1, 0))
        backward = [(target, source) for source, target in forward]
        low = lax.ppermute(
            lax.slice_in_dim(block, block.shape[dim] - width, None, axis=dim), axis, forward
        )
        high = lax.ppermute(lax.slice_in_dim(block, 0, width, axis=dim), axis, backward)
        block = jnp.concatenate([low, block, high], axis=dim)
    return block


def column_rows(inputs, layers):
    hidden = inputs
    for matrix, shift in layers[:-1]:
        pre = jnp.dot(hidden, matrix, preferred_element_type=jnp.float32) + shift[None, :]
        hidden = jax.nn.gelu(pre).astype(jnp.bfloat16)
    matrix, shift = layers[-1]
    return jnp.dot(hidden, matrix, preferred_element_type=jnp.float32) + shift[None, :]


def body(
    state,
    forcing,
    conv_weight,
    w_first,
    b_first,
    w_second,
    b_second,
    w_third,
    b_third,
    w_final,
    b_final,
    active,
    owner,
    slot,
    source,
):
    chans, rows, cols = state.shape
    wide = with_halo(state, (("lon", 2),), 1, True)
    framed = with_halo(wide, (("lat", 1),), 1, False)
    total = jnp.zeros((chans, rows, cols), jnp.float32)
    for tap in range(9):
        row_off, col_off = (tap // 3, tap % 3)
        total = total + jnp.einsum(
            "oc,cyx->oyx",
            conv_weight[tap],
            framed[:, row_off : row_off + rows, col_off : col_off + cols],
            preferred_element_type=jnp.float32,
        )
    dyn = (state.astype(jnp.float32) + total).astype(jnp.bfloat16)
    cells = rows * cols
    feat_rows = jnp.concatenate(
        [dyn.reshape(chans, cells), forcing.reshape(forcing.shape[0], cells)], axis=0
    ).T
    width_in = feat_rows.shape[1]
    feat_rows = jnp.concatenate([feat_rows, jnp.zeros((1, width_in), jnp.bfloat16)], axis=0)
    owners = lax.axis_size("lon")
    capacity = SLOTS_DEV // owners
    anchor = source.reshape(SLOTS_DEV)
    buffer = feat_rows[anchor]
    flags = (anchor < cells).astype(jnp.float32)
    act = active.reshape(cells)
    place = jnp.where(act == 1, owner.reshape(cells) * capacity + slot.reshape(cells), 0)
    layers = ((w_first, b_first), (w_second, b_second), (w_third, b_third), (w_final, b_final))
    phys = column_rows(buffer, layers)
    back = phys[:, :chans].astype(jnp.bfloat16)
    local_diag = (
        (phys[:, chans:] * flags[:, None]).astype(jnp.bfloat16).reshape(owners, capacity, chans)
    )
    diag = lax.all_to_all(local_diag, "lon", split_axis=0, concat_axis=0, tiled=True)
    tend_cells = back[place].astype(jnp.float32) * act.astype(jnp.float32)[:, None]
    new_state = (dyn.astype(jnp.float32) + tend_cells.T.reshape(chans, rows, cols)).astype(
        jnp.bfloat16
    )
    owned = diag.transpose(2, 0, 1).reshape(chans, 1, 1, owners, capacity)
    return (new_state, owned)


def solution(mesh):
    return jax.shard_map(
        body,
        mesh=mesh,
        in_specs=(
            P(None, "lat", "lon"),
            P(None, "lat", "lon"),
            P(),
            P(),
            P(),
            P(),
            P(),
            P(),
            P(),
            P(),
            P(),
            P("lat", "lon"),
            P("lat", "lon"),
            P("lat", "lon"),
            P("lat", "lon", None),
        ),
        out_specs=(P(None, "lat", "lon"), P(None, "lat", "lon", None, None)),
        check_vma=False,
    )
```

profile of v0, /device:TPU:9, one launch (start us, length us, event | category | flops | bytes accessed | tf_op | source)
XLA Modules:
  0.0 192.0 jit_solution(4577150806281507823)
XLA Ops:
  0.6 0.0 copy-start
  0.6 0.0 copy-start.3
  0.7 2.1 %copy.41 = bf16[64,32,384]{2,0,1:T(8,128)(2,1)S(1)} copy(bf16[64,32,384]{2,1,0:T(8,128)(2,1)} %param.15) | data formatting | bytes 3145728 | tf_op args[0]
  2.8 0.0 copy-start.11
  2.8 0.0 copy-start.12
  2.8 0.0 copy-start.13
  2.8 1.2 fusion.73
  4.0 2.2 %collective-permute-start = (bf16[64,32,1]{2,0,1:T(8,128)(2,1)}, bf16[64,32,1]{2,0,1:T(8,128)(2,1)S(1)}, u32[]{:S(2)}, u32[]{:S(2)}) collective-permute-start(bf16[64,32,1]{2,0,1:T(8,128)(2,1)} %get-tuple-element.12), channel_id=1, source_target_pairs={{0,1},{1,2},{2,3},{3,4},{4,5},{5,6},{6,7},{7,8},{8,9},{9,10},{10,1... | collective-permute-start | bytes 12296 | tf_op jit(solution)/shard_map/ppermute | solution.py:16
  6.4 2.4 %fusion.51 = f32[64,32,384]{2,0,1:T(8,128)} fusion(bf16[9,64,64]{2,1,0:T(8,128)(2,1)S(1)} %copy-done.8, bf16[64,32,384]{2,1,0:T(8,128)(2,1)S(1)} %copy-done.3), kind=kOutput, calls=%fused_computation.81 | convolution fusion | flops 100663296 | bytes 4734976 | tf_op jit(solution)/shard_map/oc,cyx->oyx/dot_general | solution.py:56
  8.7 0.1 copy.62
  8.8 0.1 compare_select_fusion
  8.9 4.6 %copy.49 = bf16[64,32,384]{0,2,1:T(8,128)(2,1)} copy(bf16[64,32,384]{2,1,0:T(8,128)(2,1)} %param.16) | data formatting | bytes 3145728 | tf_op args[1]
  13.6 1.8 collective-permute-done.1
  15.4 0.1 pad_maximum_fusion.7
  15.5 3.2 %collective-permute-start.2 = (bf16[64,1,386]{2,0,1:T(8,128)(2,1)S(1)}, bf16[64,1,386]{2,0,1:T(8,128)(2,1)S(1)}, u32[]{:S(2)}, u32[]{:S(2)}) collective-permute-start(bf16[64,1,386]{2,0,1:T(8,128)(2,1)S(1)} %get-tuple-element.10), channel_id=1, source_target_pairs={{0,32},{32,64},{64,96},{1,33},{33,65},{65,97},{2,34},{34,66},{66,9... | collective-permute-start | bytes 148232 | tf_op jit(solution)/shard_map/ppermute | solution.py:16
  18.7 2.1 %collective-permute-start.3 = (bf16[64,1,386]{2,0,1:T(8,128)(2,1)S(1)}, bf16[64,1,386]{2,0,1:T(8,128)(2,1)S(1)}, u32[]{:S(2)}, u32[]{:S(2)}) collective-permute-start(bf16[64,1,386]{2,0,1:T(8,128)(2,1)S(1)} %get-tuple-element.11), channel_id=1, source_target_pairs={{32,0},{64,32},{96,64},{33,1},{65,33},{97,65},{34,2},{66,34},{98,6... | collective-permute-start | bytes 148232 | tf_op jit(solution)/shard_map/ppermute | solution.py:19
  20.8 0.8 fusion.37
  21.6 0.7 fusion.39
  22.3 1.4 collective-permute-done.3
  23.7 3.0 %maximum_maximum_fusion = (bf16[64,33,386]{2,0,1:T(8,128)(2,1)S(1)}, bf16[64,33,386]{2,0,1:T(8,128)(2,1)S(1)}) fusion(bf16[64,32,1]{2,0,1:T(8,128)(2,1)S(1)} %collective-permute-done.1, bf16[64,32,384]{2,0,1:T(8,128)(2,1)S(1)} %copy.41, bf16[64,32,1]{2,0,1:T(8,128)(2,1)S(1)} %collective-permute-done, bf16[64,1,386]{2,0,1:T(8,128)(2,1)S(1)} %collective-permute-done.2, ...), kind=kLoop, calls=%fused_computation.45 | loop fusion | flops 13043712 | bytes 4940800 | tf_op jit(solution)/shard_map/concatenate | solution.py:20
  26.7 2.4 %fusion.33 = f32[32,384,64]{1,2,0:T(8,128)} fusion(bf16[64,33,386]{2,0,1:T(8,128)(2,1)S(1)} %get-tuple-element.9, bf16[9,64,64]{2,1,0:T(8,128)(2,1)S(1)} %copy-done.8), kind=kOutput, calls=%fused_computation.51 | convolution fusion | flops 100663296 | bytes 4734976 | tf_op jit(solution)/shard_map/oc,cyx->oyx/dot_general | solution.py:56
  29.0 2.2 %fusion.35 = f32[32,384,64]{1,2,0:T(8,128)} fusion(bf16[64,33,386]{2,0,1:T(8,128)(2,1)S(1)} %get-tuple-element.9, bf16[9,64,64]{2,1,0:T(8,128)(2,1)S(1)} %copy-done.8), kind=kOutput, calls=%fused_computation.53 | convolution fusion | flops 100663296 | bytes 4734976 | tf_op jit(solution)/shard_map/oc,cyx->oyx/dot_general | solution.py:56
  31.3 2.3 %fusion.41 = f32[32,384,64]{1,2,0:T(8,128)} fusion(bf16[64,33,386]{2,0,1:T(8,128)(2,1)S(1)} %get-tuple-element.8, bf16[9,64,64]{2,1,0:T(8,128)(2,1)S(1)} %copy-done.8), kind=kOutput, calls=%fused_computation.61 | convolution fusion | flops 100663296 | bytes 4734976 | tf_op jit(solution)/shard_map/oc,cyx->oyx/dot_general | solution.py:56
  33.6 2.4 %fusion.43 = f32[32,384,64]{1,2,0:T(8,128)} fusion(bf16[64,33,386]{2,0,1:T(8,128)(2,1)S(1)} %get-tuple-element.8, bf16[9,64,64]{2,1,0:T(8,128)(2,1)S(1)} %copy-done.8), kind=kOutput, calls=%fused_computation.63 | convolution fusion | flops 100663296 | bytes 4734976 | tf_op jit(solution)/shard_map/oc,cyx->oyx/dot_general | solution.py:56
  35.9 2.2 %fusion.45 = f32[32,384,64]{1,2,0:T(8,128)} fusion(bf16[64,33,386]{2,0,1:T(8,128)(2,1)S(1)} %get-tuple-element.8, bf16[9,64,64]{2,1,0:T(8,128)(2,1)S(1)} %copy-done.8), kind=kOutput, calls=%fused_computation.65 | convolution fusion | flops 100663296 | bytes 4734976 | tf_op jit(solution)/shard_map/oc,cyx->oyx/dot_general | solution.py:56
  38.1 1.3 copy-done.7
  39.4 7.3 %fusion.30 = bf16[64,32,384]{2,0,1:T(8,128)(2,1)S(1)} fusion(f32[32,384,64]{1,2,0:T(8,128)} %fusion.33, f32[32,384,64]{1,2,0:T(8,128)} %fusion.35, f32[32,384,64]{1,2,0:T(8,128)S(1)} %fusion.37, f32[64,32,384]{2,0,1:T(8,128)S(1)} %copy-done.7, f32[32,384,64]{1,2,0:T(8,128)S(1)} %fusion.39, f32[32,384,64]{1,2,0:T(8,128)} %fusion.41, ...), kind=kOutput, calls=%fused_computation.39 | convolution fusion | flops 109314048 | bytes 29900800 | tf_op jit(solution)/shard_map/oc,cyx->oyx/dot_general | solution.py:56
  46.8 0.0 copy-start.5
  46.8 2.9 %copy.57 = bf16[64,32,384]{0,2,1:T(8,128)(2,1)} copy(bf16[64,32,384]{2,0,1:T(8,128)(2,1)S(1)} %fusion.30) | data formatting | bytes 3145728 | tf_op jit(solution)/shard_map/reshape | solution.py:65
  49.7 3.7 %maximum_bitcast_fusion = bf16[12288,128]{1,0:T(8,128)(2,1)S(1)} fusion(bf16[64,12288]{0,1:T(8,128)(2,1)} %bitcast.90, bf16[64,12288]{0,1:T(8,128)(2,1)} %bitcast.91), kind=kLoop, calls=%fused_computation.36 | loop fusion | flops 6291456 | bytes 6291456 | tf_op jit(solution)/shard_map/transpose | solution.py:66
  53.4 1.8 concatenate.32
  55.2 24.3 %gather_fusion = bf16[8192,128]{1,0:T(8,128)(2,1)S(1)} fusion(bf16[12289,128]{1,0:T(8,128)(2,1)} %concatenate.32, s32[8192]{0:T(1024)S(1)} %broadcast_clamp_fusion.1), kind=kCustom, calls=%fused_computation | custom fusion | bytes 4227072 | tf_op jit(solution)/shard_map/gather | solution.py:72
  79.5 0.0 copy-start.15
  79.5 8.0 %fusion.7 = bf16[8192,512]{1,0:T(8,128)(2,1)} fusion(bf16[8192,128]{1,0:T(8,128)(2,1)S(1)} %gather_fusion, bf16[128,512]{1,0:T(8,128)(2,1)S(1)} %copy-done.16, f32[512]{0:T(512)S(1)} %copy-done.17), kind=kOutput, calls=%fused_computation.12 | convolution fusion | flops 1115684864 | bytes 10618880 | tf_op jit(solution)/shard_map/dot_general | solution.py:27
  87.6 18.9 %fusion.23 = bf16[8192,512]{1,0:T(8,128)(2,1)} fusion(bf16[512,512]{1,0:T(8,128)(2,1)S(1)} %copy-done, bf16[8192,512]{1,0:T(8,128)(2,1)} %fusion.7, bf16[512,512]{1,0:T(8,128)(2,1)S(1)} %copy-done.15, f32[512]{0:T(512)S(1)} %copy-done.18, f32[512]{0:T(512)S(1)} %copy-done.19), kind=kOutput, calls=%fused_computation.28 | convolution fusion | flops 8673820672 | bytes 17829888 | tf_op jit(solution)/shard_map/dot_general | solution.py:27
  106.5 6.2 %convolution_add_fusion = f32[8192,128]{0,1:T(8,128)S(1)} fusion(bf16[8192,512]{1,0:T(8,128)(2,1)} %fusion.23, bf16[512,128]{1,0:T(8,128)(2,1)S(1)} %copy-done.9, f32[128]{0:T(128)S(1)} %copy-done.14), kind=kOutput, calls=%fused_computation.29 | convolution fusion | flops 1074790400 | bytes 12714496 | tf_op jit(solution)/shard_map/dot_general | solution.py:30
  112.7 1.9 %copy-done.2 = f32[8192,128]{0,1:T(8,128)} copy-done((f32[8192,128]{0,1:T(8,128)}, f32[8192,128]{0,1:T(8,128)S(1)}, u32[]{:S(2)}) %copy-start.2) | copy-done | bytes 4194328
  114.7 1.1 slice.167
  115.7 2.0 %copy.51 = bf16[8192,64]{1,0:T(8,128)(2,1)S(1)} copy(bf16[8192,64]{0,1:T(8,128)(2,1)} %slice.167) | data formatting | bytes 2097152 | tf_op jit(solution)/shard_map/slice | solution.py:78
  117.8 1.7 fusion.31
  119.5 1.1 copy.67
  120.6 8.6 %all-to-all-start = ((bf16[32,256,64]{1,2,0:T(8,128)(2,1)}), bf16[32,256,64]{1,2,0:T(8,128)(2,1)}, u32[]{:S(2)}, u32[]{:S(2)}) async-start(bf16[32,256,64]{1,2,0:T(8,128)(2,1)} %bitcast.93), calls=%async_computation | async-start | bytes 2097152 | tf_op jit(solution)/shard_map/all_to_all | solution.py:82
  129.3 43.3 %gather_fusion.1 = bf16[12288,64]{1,0:T(8,128)(2,1)} fusion(bf16[8192,64]{1,0:T(8,128)(2,1)S(1)} %copy.51, s32[12288]{0:T(1024)S(1)} %broadcast_clamp_fusion), kind=kCustom, calls=%fused_computation.1 | custom fusion | bytes 3194880 | tf_op jit(solution)/shard_map/gather | solution.py:83
  172.5 5.8 %convert_multiply_fusion = f32[12288,64]{1,0:T(8,128)} fusion(bf16[12288,64]{1,0:T(8,128)(2,1)} %gather_fusion.1, f32[12288]{0:T(1024)S(1)} %convert_element_type.58), kind=kLoop, calls=%fused_computation.35 | loop fusion | flops 1572864 | bytes 4767744 | tf_op jit(solution)/shard_map/mul | solution.py:83
  178.3 6.3 %copy.53 = f32[64,32,384]{2,0,1:T(8,128)} copy(f32[64,32,384]{0,2,1:T(8,128)} %bitcast.89) | data formatting | bytes 6291456 | tf_op jit(solution)/shard_map/reshape | solution.py:84
  184.7 2.4 %add_convert_fusion = bf16[64,32,384]{2,0,1:T(8,128)(2,1)S(1)} fusion(f32[64,32,384]{2,0,1:T(8,128)} %copy.53, bf16[64,32,384]{2,0,1:T(8,128)(2,1)S(1)} %copy-done.6), kind=kLoop, calls=%fused_computation.44 | loop fusion | flops 2359296 | bytes 6291456 | tf_op jit(solution)/shard_map/convert_element_type | solution.py:84
  187.1 2.1 %copy.55 = bf16[64,32,384]{2,1,0:T(8,128)(2,1)} copy(bf16[64,32,384]{2,0,1:T(8,128)(2,1)S(1)} %add_convert_fusion) | data formatting | bytes 3145728
  189.2 2.8 %copy.56 = bf16[64,1,1,32,256]{4,3,2,1,0:T(8,128)(2,1)} copy(bf16[64,1,1,32,256]{4,0,3,2,1:T(8,128)(2,1)} %bitcast.33) | data formatting | bytes 2097152
  (41 shorter events, 0.2 us)
Async XLA Ops:
  0.6 86.9 %copy-start = (bf16[512,512]{1,0:T(8,128)(2,1)S(1)}, bf16[512,512]{1,0:T(8,128)(2,1)}, u32[]{:S(2)}) copy-start(bf16[512,512]{1,0:T(8,128)(2,1)} %param.22) | copy-start | bytes 1572868
  0.6 5.7 %copy-start.3 = (bf16[64,32,384]{2,1,0:T(8,128)(2,1)S(1)}, bf16[64,32,384]{2,1,0:T(8,128)(2,1)}, u32[]{:S(2)}) copy-start(bf16[64,32,384]{2,1,0:T(8,128)(2,1)} %param.15) | copy-start | bytes 4718596
  0.7 5.6 %copy-start.10 = (s32[1,1,8192]{2,1,0:T(1,128)S(1)}, s32[1,1,8192]{2,1,0:T(1,128)}, u32[]{:S(2)}) copy-start(s32[1,1,8192]{2,1,0:T(1,128)} %param.29) | copy-start | bytes 98308
  0.7 5.7 %copy-start.8 = (bf16[9,64,64]{2,1,0:T(8,128)(2,1)S(1)}, bf16[9,64,64]{2,1,0:T(8,128)(2,1)}, u32[]{:S(2)}) copy-start(bf16[9,64,64]{2,1,0:T(8,128)(2,1)} %param.17) | copy-start | bytes 221188
  2.8 5.9 %copy-start.11 = (s32[32,384]{1,0:T(8,128)S(1)}, s32[32,384]{1,0:T(8,128)}, u32[]{:S(2)}) copy-start(s32[32,384]{1,0:T(8,128)} %param.26) | copy-start | bytes 147460
  2.8 5.9 %copy-start.12 = (s32[32,384]{1,0:T(8,128)S(1)}, s32[32,384]{1,0:T(8,128)}, u32[]{:S(2)}) copy-start(s32[32,384]{1,0:T(8,128)} %param.28) | copy-start | bytes 147460
  2.8 5.9 %copy-start.13 = (s32[32,384]{1,0:T(8,128)S(1)}, s32[32,384]{1,0:T(8,128)}, u32[]{:S(2)}) copy-start(s32[32,384]{1,0:T(8,128)} %param.27) | copy-start | bytes 147460
  4.0 9.5 %collective-permute-start = (bf16[64,32,1]{2,0,1:T(8,128)(2,1)}, bf16[64,32,1]{2,0,1:T(8,128)(2,1)S(1)}, u32[]{:S(2)}, u32[]{:S(2)}) collective-permute-start(bf16[64,32,1]{2,0,1:T(8,128)(2,1)} %get-tuple-element.12), channel_id=1, source_target_pairs={{0,1},{1,2},{2,3},{3,4},{4,5},{5,6},{6,7},{7,8},{8,9},{9,10},{10,1... | collective-permute-start | bytes 12296 | tf_op jit(solution)/shard_map/ppermute | solution.py:16
  6.2 9.1 %collective-permute-start.1 = (bf16[64,32,1]{2,0,1:T(8,128)(2,1)}, bf16[64,32,1]{2,0,1:T(8,128)(2,1)S(1)}, u32[]{:S(2)}, u32[]{:S(2)}) collective-permute-start(bf16[64,32,1]{2,0,1:T(8,128)(2,1)} %get-tuple-element.13), channel_id=1, source_target_pairs={{1,0},{2,1},{3,2},{4,3},{5,4},{6,5},{7,6},{8,7},{9,8},{10,9},{11,1... | collective-permute-start | bytes 12296 | tf_op jit(solution)/shard_map/ppermute | solution.py:19
  15.5 6.8 %collective-permute-start.2 = (bf16[64,1,386]{2,0,1:T(8,128)(2,1)S(1)}, bf16[64,1,386]{2,0,1:T(8,128)(2,1)S(1)}, u32[]{:S(2)}, u32[]{:S(2)}) collective-permute-start(bf16[64,1,386]{2,0,1:T(8,128)(2,1)S(1)} %get-tuple-element.10), channel_id=1, source_target_pairs={{0,32},{32,64},{64,96},{1,33},{33,65},{65,97},{2,34},{34,66},{66,9... | collective-permute-start | bytes 148232 | tf_op jit(solution)/shard_map/ppermute | solution.py:16
  18.7 5.0 %collective-permute-start.3 = (bf16[64,1,386]{2,0,1:T(8,128)(2,1)S(1)}, bf16[64,1,386]{2,0,1:T(8,128)(2,1)S(1)}, u32[]{:S(2)}, u32[]{:S(2)}) collective-permute-start(bf16[64,1,386]{2,0,1:T(8,128)(2,1)S(1)} %get-tuple-element.11), channel_id=1, source_target_pairs={{32,0},{64,32},{96,64},{33,1},{65,33},{97,65},{34,2},{66,34},{98,6... | collective-permute-start | bytes 148232 | tf_op jit(solution)/shard_map/ppermute | solution.py:19
  35.9 2.2 %copy-start.4 = (bf16[64,32,384]{2,1,0:T(8,128)(2,1)S(1)}, bf16[64,32,384]{2,1,0:T(8,128)(2,1)}, u32[]{:S(2)}) copy-start(bf16[64,32,384]{2,1,0:T(8,128)(2,1)} %param.15) | copy-start | bytes 4718596
  35.9 3.5 %copy-start.7 = (f32[64,32,384]{2,0,1:T(8,128)S(1)}, f32[64,32,384]{2,0,1:T(8,128)}, u32[]{:S(2)}) copy-start(f32[64,32,384]{2,0,1:T(8,128)} %fusion.51) | copy-start | bytes 9437188
  46.8 6.6 %copy-start.5 = (bf16[64,32,384]{2,0,1:T(8,128)(2,1)}, bf16[64,32,384]{2,0,1:T(8,128)(2,1)S(1)}, u32[]{:S(2)}) copy-start(bf16[64,32,384]{2,0,1:T(8,128)(2,1)S(1)} %fusion.30) | copy-start | bytes 4718596
  55.2 24.3 %copy-start.16 = (bf16[128,512]{1,0:T(8,128)(2,1)S(1)}, bf16[128,512]{1,0:T(8,128)(2,1)}, u32[]{:S(2)}) copy-start(bf16[128,512]{1,0:T(8,128)(2,1)} %param.18) | copy-start | bytes 393220
  55.2 24.3 %copy-start.17 = (f32[512]{0:T(512)S(1)}, f32[512]{0:T(512)}, u32[]{:S(2)}) copy-start(f32[512]{0:T(512)} %param.19) | copy-start | bytes 6148
  79.5 8.1 %copy-start.15 = (bf16[512,512]{1,0:T(8,128)(2,1)S(1)}, bf16[512,512]{1,0:T(8,128)(2,1)}, u32[]{:S(2)}) copy-start(bf16[512,512]{1,0:T(8,128)(2,1)} %param.20) | copy-start | bytes 1572868
  79.5 8.1 %copy-start.18 = (f32[512]{0:T(512)S(1)}, f32[512]{0:T(512)}, u32[]{:S(2)}) copy-start(f32[512]{0:T(512)} %param.23) | copy-start | bytes 6148
  79.5 8.1 %copy-start.19 = (f32[512]{0:T(512)S(1)}, f32[512]{0:T(512)}, u32[]{:S(2)}) copy-start(f32[512]{0:T(512)} %param.21) | copy-start | bytes 6148
  87.6 18.9 %copy-start.9 = (bf16[512,128]{1,0:T(8,128)(2,1)S(1)}, bf16[512,128]{1,0:T(8,128)(2,1)}, u32[]{:S(2)}) copy-start(bf16[512,128]{1,0:T(8,128)(2,1)} %param.24) | copy-start | bytes 393220
  87.6 18.9 %copy-start.14 = (f32[128]{0:T(128)S(1)}, f32[128]{0:T(128)}, u32[]{:S(2)}) copy-start(f32[128]{0:T(128)} %param.25) | copy-start | bytes 1540
  112.7 2.0 %copy-start.2 = (f32[8192,128]{0,1:T(8,128)}, f32[8192,128]{0,1:T(8,128)S(1)}, u32[]{:S(2)}) copy-start(f32[8192,128]{0,1:T(8,128)S(1)} %convolution_add_fusion) | copy-start | bytes 12582916
  120.6 68.6 %all-to-all-start = ((bf16[32,256,64]{1,2,0:T(8,128)(2,1)}), bf16[32,256,64]{1,2,0:T(8,128)(2,1)}, u32[]{:S(2)}, u32[]{:S(2)}) async-start(bf16[32,256,64]{1,2,0:T(8,128)(2,1)} %bitcast.93), calls=%async_computation | async-start | bytes 2097152 | tf_op jit(solution)/shard_map/all_to_all | solution.py:82
  178.3 6.3 %copy-start.6 = (bf16[64,32,384]{2,0,1:T(8,128)(2,1)S(1)}, bf16[64,32,384]{2,0,1:T(8,128)(2,1)}, u32[]{:S(2)}) copy-start(bf16[64,32,384]{2,0,1:T(8,128)(2,1)} %copy-done.5) | copy-start | bytes 4718596
  184.7 7.3 %copy-start.1 = (bf16[512,512]{1,0:T(8,128)(2,1)S(1)}, bf16[512,512]{1,0:T(8,128)(2,1)}, u32[]{:S(2)}) copy-start(bf16[512,512]{1,0:T(8,128)(2,1)} %param.22) | copy-start | bytes 1572868
where the time goes:
time: 193 us; the launch traced here: 192 us
  local copies, waits for them, and re-layouts  99 us (51%)
  matrix products  55.8 us (29%)
  other arithmetic  16.9 us (9%)
  starting transfers between devices  16.1 us (8%)
  waiting for transfers between devices  3.21 us (2%)
    gather x1, local copies, waits for them, and re-layouts, body(): back[place].astype(jnp.float32) * act.astype(jnp.float32)[:, None]  43.3 us
    dot_general x3, matrix products, column_rows(): jnp.dot(hidden, matrix, preferred_element_type=jnp.float32) + shift[None, :]  33.2 us
    gather x1, local copies, waits for them, and re-layouts, body(): buffer = feat_rows[anchor]  24.3 us
    dot_general x9, matrix products, body(): jnp.einsum('oc,cyx->oyx', conv_weight[tap], framed[:, row_off:row_off + r...  22.7 us
    unnamed x45, local copies, waits for them, and re-layouts  15 us
    all_to_all x1, starting transfers between devices, body(): lax.all_to_all(local_diag, 'lon', split_axis=0, concat_axis=0, tiled=True)  8.64 us
    reshape x1, local copies, waits for them, and re-layouts, body(): tend_cells.T.reshape(chans, rows, cols)  6.33 us
    mul x1, other arithmetic, body(): back[place].astype(jnp.float32) * act.astype(jnp.float32)[:, None]  5.79 us
  transfers between devices with their start and end apart: 5, of which 2 were waited for; matrix products, arithmetic and copies ran while one was open for 36% of the time, Pallas kernels for 0%

commit v1 on v0

v1 whole, which is shorter than its diff:
```python
import functools

import jax
import jax.numpy as jnp
from jax import lax
from jax.experimental import pallas as pl
from jax.experimental.pallas import tpu as pltpu
from jax.sharding import PartitionSpec as P

K0 = 0.7978845608028654
K1 = K0 * 0.044715
SUB = 128
GROUP = 4


def half_gelu(y):
    t = jnp.tanh(y * (2.0 * K0 + (8.0 * K1) * (y * y)))
    return y + y * t


def active_blocks(src, table, cells, blocks):
    def scan(b, n):
        table[n] = b
        return n + (src[b * SUB] < cells).astype(jnp.int32)

    count = lax.fori_loop(0, blocks, scan, jnp.int32(0))
    last = table[jnp.maximum(count - 1, 0)]
    last = jnp.where(count > 0, last, 0)
    for extra in range(GROUP):
        table[count + extra] = last
    return count


def columns_kernel(
    src, s_ref, e_ref, top_ref, bot_ref, f_ref, cw_ref, w1_ref, b1_ref, w2_ref, b2_ref,
    w3_ref, b3_ref, w4_ref, b4_ref, vsrc_ref,
    dyn_ref, tend_ref, send_ref,
    ext, feats, xbuf, w1h, w2h, w3h, table,
):
    rows, chans, cols = s_ref.shape
    cells = rows * cols
    blocks = vsrc_ref.shape[0]
    wide = cols + 128
    ext[0] = top_ref[...]
    ext[rows + 1] = bot_ref[...]
    ext[1 : rows + 1, :, :cols] = s_ref[...]
    ext[1 : rows + 1, :, cols:] = e_ref[...]
    feats[cells : cells + 8, :] = jnp.zeros((8, 2 * chans), jnp.float32)
    w1h[...] = w1_ref[...] * jnp.bfloat16(0.5)
    w2h[...] = w2_ref[...] * jnp.bfloat16(0.5)
    w3h[...] = w3_ref[...] * jnp.bfloat16(0.5)
    send_ref[...] = jnp.zeros(send_ref.shape, send_ref.dtype)

    def conv_row(y, carry):
        x = ext[pl.ds(y, 3)].reshape(3 * chans, wide)
        p = jnp.dot(cw_ref[...], x, preferred_element_type=jnp.float32)
        total = (
            s_ref[y].astype(jnp.float32)
            + p[chans : 2 * chans, :cols]
            + pltpu.roll(p[:chans], 1, 1)[:, :cols]
            + pltpu.roll(p[2 * chans :], wide - 1, 1)[:, :cols]
        )
        dyn = total.astype(jnp.bfloat16)
        dyn_ref[y] = dyn
        both = jnp.concatenate([dyn.astype(jnp.float32), f_ref[y].astype(jnp.float32)], axis=0)
        feats[pl.ds(pl.multiple_of(y * cols, 128), cols), :] = both.T
        return carry

    lax.fori_loop(0, rows, conv_row, 0)

    count = active_blocks(src, table, cells, blocks)

    def group(g, carry):
        for j in range(GROUP):
            base = table[g * GROUP + j] * SUB

            def fetch(i, c, base=base, j=j):
                for r in range(16):
                    at = src[base + i * 16 + r]
                    xbuf[pl.ds(j * SUB + i * 16 + r, 1), :] = feats[pl.ds(at, 1), :]
                return c

            lax.fori_loop(0, SUB // 16, fetch, 0)
        h = xbuf[...].astype(jnp.bfloat16)
        for w, b in ((w1h, b1_ref), (w2h, b2_ref), (w3h, b3_ref)):
            pre = jnp.dot(h, w[...], preferred_element_type=jnp.float32) + b[...] * 0.5
            h = half_gelu(pre).astype(jnp.bfloat16)
        out = jnp.dot(h, w4_ref[...], preferred_element_type=jnp.float32) + b4_ref[...]
        for j in range(GROUP):
            blk = table[g * GROUP + j]
            part = out[j * SUB : (j + 1) * SUB]
            tend_ref[pl.ds(pl.multiple_of(blk * SUB, SUB), SUB), :] = part.astype(jnp.bfloat16)
            ok = vsrc_ref[pl.ds(blk, 1), :] < cells
            diag = jnp.where(ok, part.T[chans:], 0.0)
            send_ref[blk] = diag.astype(jnp.bfloat16)
        return carry

    lax.fori_loop(0, (count + GROUP - 1) // GROUP, group, 0)


def place_kernel(src, dyn_ref, tend_ref, new_ref, acc, rbuf, table):
    rows, chans, cols = dyn_ref.shape
    cells = rows * cols
    blocks = tend_ref.shape[0] // SUB

    acc[...] = jnp.zeros(acc.shape, jnp.float32)
    count = active_blocks(src, table, cells, blocks)

    def block(n, carry):
        base = table[n] * SUB
        rbuf[...] = tend_ref[pl.ds(pl.multiple_of(base, SUB), SUB), :].astype(jnp.float32)

        def put(i, c):
            for r in range(16):
                at = src[base + i * 16 + r]
                acc[pl.ds(at, 1), :] = rbuf[pl.ds(i * 16 + r, 1), :]
            return c

        lax.fori_loop(0, SUB // 16, put, 0)
        return carry

    lax.fori_loop(0, count, block, 0)

    def row(y, carry):
        part = acc[pl.ds(pl.multiple_of(y * cols, 128), cols), :].T[:chans]
        new_ref[y] = (dyn_ref[y].astype(jnp.float32) + part).astype(jnp.bfloat16)
        return carry

    lax.fori_loop(0, rows, row, 0)


def shift(block, axis, step, periodic):
    count = lax.axis_size(axis)
    pairs = [(i, (i + step) % count) for i in range(count) if periodic or 0 <= i + step < count]
    return lax.ppermute(block, axis, pairs)


def body(
    state, forcing, conv_weight, w_first, b_first, w_second, b_second, w_third, b_third,
    w_final, b_final, active, owner, slot, source,
):
    chans, rows, cols = state.shape
    slots = source.size
    blocks = slots // SUB
    cells = rows * cols
    hid = w_second.shape[0]
    src = source.reshape(slots)

    s = state.transpose(1, 0, 2)
    left = shift(s[:, :, cols - 1 :], "lon", 1, True)
    right = shift(s[:, :, :1], "lon", -1, True)
    f = forcing.transpose(1, 0, 2)
    cw = conv_weight.reshape(3, 3, chans, chans).transpose(1, 2, 0, 3).reshape(3 * chans, 3 * chans)
    edge = jnp.concatenate([right, jnp.zeros((rows, chans, 126), jnp.bfloat16), left], axis=2)
    top = shift(jnp.concatenate([s[-1], edge[-1]], axis=1), "lat", 1, False)
    bot = shift(jnp.concatenate([s[0], edge[0]], axis=1), "lat", -1, False)

    vmem = pl.BlockSpec(memory_space=pltpu.VMEM)
    smem = pl.BlockSpec(memory_space=pltpu.SMEM)
    dyn, tend, send = pl.pallas_call(
        columns_kernel,
        out_shape=(
            jax.ShapeDtypeStruct((rows, chans, cols), jnp.bfloat16),
            jax.ShapeDtypeStruct((slots, 2 * chans), jnp.bfloat16),
            jax.ShapeDtypeStruct((blocks, chans, SUB), jnp.bfloat16),
        ),
        in_specs=[smem] + [vmem] * 15,
        out_specs=(vmem, vmem, vmem),
        scratch_shapes=[
            pltpu.VMEM((rows + 2, chans, cols + 128), jnp.bfloat16),
            pltpu.VMEM((cells + 8, 2 * chans), jnp.float32),
            pltpu.VMEM((GROUP * SUB, 2 * chans), jnp.float32),
            pltpu.VMEM(w_first.shape, jnp.bfloat16),
            pltpu.VMEM(w_second.shape, jnp.bfloat16),
            pltpu.VMEM(w_third.shape, jnp.bfloat16),
            pltpu.SMEM((blocks + GROUP + 4,), jnp.int32),
        ],
        compiler_params=pltpu.CompilerParams(vmem_limit_bytes=48 << 20),
        cost_estimate=pl.CostEstimate(flops=10_000_000_000, bytes_accessed=8_000_000, transcendentals=8_000_000),
        name="columns",
    )(
        src, s, edge, top, bot, f, cw, w_first, b_first.reshape(1, hid), w_second,
        b_second.reshape(1, hid), w_third, b_third.reshape(1, hid), w_final,
        b_final.reshape(1, 2 * chans), src.reshape(blocks, SUB),
    )
    got = lax.all_to_all(send, "lon", split_axis=0, concat_axis=0, tiled=True)
    new = pl.pallas_call(
        place_kernel,
        out_shape=jax.ShapeDtypeStruct((rows, chans, cols), jnp.bfloat16),
        in_specs=[smem, vmem, vmem],
        out_specs=vmem,
        scratch_shapes=[
            pltpu.VMEM((cells + 8, 2 * chans), jnp.float32),
            pltpu.VMEM((SUB, 2 * chans), jnp.float32),
            pltpu.SMEM((blocks + GROUP + 4,), jnp.int32),
        ],
        compiler_params=pltpu.CompilerParams(vmem_limit_bytes=32 << 20),
        cost_estimate=pl.CostEstimate(flops=5_000_000_000, bytes_accessed=8_000_000, transcendentals=0),
        name="place",
    )(src, dyn, tend)
    new_state = new.transpose(1, 0, 2)
    owners = lax.axis_size("lon")
    halves = blocks // owners
    owned = got.reshape(owners, halves, chans, SUB).transpose(2, 0, 1, 3).reshape(chans, 1, 1, owners, halves * SUB)
    return (new_state, owned)


def solution(mesh):
    field = P(None, "lat", "lon")
    return jax.shard_map(
        body,
        mesh=mesh,
        in_specs=(field, field) + (P(),) * 9 + (P("lat", "lon"),) * 3 + (P("lat", "lon", None),),
        out_specs=(field, P(None, "lat", "lon", None, None)),
        check_vma=False,
    )
```

time: 193 us -> 103 us (0.53)
  local copies, waits for them, and re-layouts: 99 us -> 12.8 us
  Pallas kernels: 0 us -> 60.7 us
  matrix products: 55.8 us -> 0 us
  other arithmetic: 16.9 us -> 0.34 us
  waiting for transfers between devices: 3.21 us -> 7.7 us
  starting transfers between devices: 16.1 us -> 18.8 us
    gather x2 -> x0, local copies, waits for them, and re-layouts: 67.6 us -> none  [the longest x1 43.3 us: body(): back[place].astype(jnp.float32) * act.astype(jnp.float32)[:, None]]
    pallas_call x0 -> x2, Pallas kernels: none -> 60.7 us  [the longest x1 45.9 us: body(): pl.pallas_call(columns_kernel, out_shape=(jax.ShapeDtypeStruct((rows, cha...]
    dot_general x12 -> x0, matrix products: 55.8 us -> none  [the longest x3 33.2 us: column_rows(): jnp.dot(hidden, matrix, preferred_element_type=jnp.float32) + shift[None, :]]
    reshape x3, local copies, waits for them, and re-layouts: 10.3 us -> 1.78 us  [the longest x1 1.49 us: body(): got.reshape(owners, halves, chans, SUB).transpose(2, 0, 1, 3)]
    unnamed x45 -> x33, local copies, waits for them, and re-layouts: 15 us -> 8.32 us
    mul x1 -> x0, other arithmetic: 5.79 us -> none  [body(): back[place].astype(jnp.float32) * act.astype(jnp.float32)[:, None]]
    ppermute x4, waiting for transfers between devices: 3.2 us -> 7.7 us  [shift(): return lax.ppermute(block, axis, pairs)]
    convert_element_type x4 -> x0, other arithmetic: 4.21 us -> none  [the longest x1 2.44 us: body(): (dyn.astype(jnp.float32) + tend_cells.T.reshape(chans, rows, cols)).astyp...]
  transfers between devices with their start and end apart: 5 -> 5, of which waited for: 2 -> 2; matrix products, arithmetic and copies ran while one was open for 36% -> 4% of each run, Pallas kernels for 0% -> 15%
where the time goes in v1:
time: 103 us; the launch traced here: 101 us
  Pallas kernels  60.7 us (59%)
  starting transfers between devices  18.8 us (18%)
  local copies, waits for them, and re-layouts  12.8 us (12%)
  waiting for transfers between devices  7.7 us (7%)
    pallas_call x1, Pallas kernels, body(): pl.pallas_call(columns_kernel, out_shape=(jax.ShapeDtypeStruct((rows, cha...  45.9 us
    pallas_call x1, Pallas kernels, body(): pl.pallas_call(place_kernel, out_shape=jax.ShapeDtypeStruct((rows, chans,...  14.8 us
    all_to_all x1, starting transfers between devices, body(): got = lax.all_to_all(send, 'lon', split_axis=0, concat_axis=0, tiled=True)  11.2 us
    unnamed x33, local copies, waits for them, and re-layouts  8.32 us
    ppermute x4, waiting for transfers between devices, shift(): return lax.ppermute(block, axis, pairs)  7.7 us
    ppermute x4, starting transfers between devices, shift(): return lax.ppermute(block, axis, pairs)  7.63 us
    transpose x1, local copies, waits for them, and re-layouts, body(): got.reshape(owners, halves, chans, SUB).transpose(2, 0, 1, 3)  2.3 us
  transfers between devices with their start and end apart: 5, of which 2 were waited for; matrix products, arithmetic and copies ran while one was open for 4% of the time, Pallas kernels for 15%

profile of v1, /device:TPU:9, one launch (start us, length us, event | category | flops | bytes accessed | tf_op | source)
XLA Modules:
  0.0 101.2 jit_solution(14156639491539348145)
XLA Ops:
  0.6 2.0 %copy.28 = bf16[64,32,384]{2,0,1:T(8,128)(2,1)S(1)} copy(bf16[64,32,384]{2,1,0:T(8,128)(2,1)} %param.15) | data formatting | bytes 3145728 | tf_op args[0]
  2.6 0.0 copy-start.12
  2.6 0.3 fusion
  2.9 0.0 copy-start.14
  2.9 0.0 copy-start.13
  2.9 0.7 collective-permute-start
  3.6 1.6 %collective-permute-start.1 = (bf16[32,64,1]{2,1,0:T(8,128)(2,1)S(1)}, bf16[32,64,1]{2,1,0:T(8,128)(2,1)S(1)}, u32[]{:S(2)}, u32[]{:S(2)}) collective-permute-start(bf16[32,64,1]{2,1,0:T(8,128)(2,1)S(1)} %get-tuple-element.15), channel_id=1, source_target_pairs={{0,1},{1,2},{2,3},{3,4},{4,5},{5,6},{6,7},{7,8},{8,9},{9,10},{10,1... | collective-permute-start | bytes 12296 | tf_op jit(solution)/shard_map/ppermute | solution.py:135
  5.3 0.1 pad.5.clone
  5.3 6.7 %collective-permute-done = bf16[32,64,1]{2,1,0:T(8,128)(2,1)S(1)} collective-permute-done((bf16[32,64,1]{2,1,0:T(8,128)(2,1)S(1)}, bf16[32,64,1]{2,1,0:T(8,128)(2,1)S(1)}, u32[]{:S(2)}, u32[]{:S(2)}) %collective-permute-start) | collective-permute-done | bytes 4128 | tf_op jit(solution)/shard_map/ppermute | solution.py:135
  12.0 0.0 collective-permute-done.1
  12.0 0.3 pad_maximum_fusion.e_ref
  12.4 0.0 copy-done.12
  12.4 3.2 %collective-permute-start.2 = (bf16[64,512]{1,0:T(8,128)(2,1)S(1)}, bf16[64,512]{1,0:T(8,128)(2,1)S(1)}, u32[]{:S(2)}, u32[]{:S(2)}) collective-permute-start(bf16[64,512]{1,0:T(8,128)(2,1)S(1)} %pad_maximum_fusion.1), channel_id=1, source_target_pairs={{0,32},{32,64},{64,96},{1,33},{33,65},{65,97},{2,34},{34,66},{66,9... | collective-permute-start | bytes 196616 | tf_op jit(solution)/shard_map/ppermute | solution.py:135
  15.6 2.1 %collective-permute-start.3 = (bf16[64,512]{1,0:T(8,128)(2,1)S(1)}, bf16[64,512]{1,0:T(8,128)(2,1)S(1)}, u32[]{:S(2)}, u32[]{:S(2)}) collective-permute-start(bf16[64,512]{1,0:T(8,128)(2,1)S(1)} %pad_maximum_fusion.2), channel_id=1, source_target_pairs={{32,0},{64,32},{96,64},{33,1},{65,33},{97,65},{34,2},{66,34},{98,6... | collective-permute-start | bytes 196616 | tf_op jit(solution)/shard_map/ppermute | solution.py:135
  17.7 0.0 copy-done.14
  17.7 0.1 copy.29
  17.9 0.2 reshape.33.cw_ref
  18.0 0.0 copy-done.13
  18.0 0.0 copy-start
  18.0 0.0 copy-start.1
  18.1 0.0 copy-start.2
  18.1 0.0 copy-start.3
  18.1 0.0 copy-start.4
  18.1 0.0 copy-start.5
  18.1 0.0 copy-start.6
  18.1 0.0 copy-start.7
  18.1 0.0 copy-start.8
  18.1 1.7 %copy.27 = bf16[64,32,384]{2,0,1:T(8,128)(2,1)} copy(bf16[64,32,384]{2,1,0:T(8,128)(2,1)S(1)} %copy-done.13) | data formatting | bytes 3145728 | tf_op args[1]
  19.8 0.0 collective-permute-done.2.top_ref
  19.8 1.0 collective-permute-done.3.bot_ref
  20.8 0.0 copy-done
  20.8 0.0 copy-done.1
  20.8 0.0 copy-done.2
  20.9 0.0 copy-done.3
  20.9 0.0 copy-done.4
  20.9 0.0 copy-done.5
  20.9 0.0 copy-done.6
  20.9 0.0 copy-done.7
  20.9 45.9 %columns.1 = (bf16[32,64,384]{2,1,0:T(8,128)(2,1)S(1)}, bf16[8192,128]{1,0:T(8,128)(2,1)}, bf16[64,64,128]{2,1,0:T(8,128)(2,1)}) custom-call(s32[8192]{0:T(1024)S(1)} %bitcast.29, bf16[32,64,384]{2,1,0:T(8,128)(2,1)} %bitcast.38, bf16[32,64,128]{2,1,0:T(8,128)(2,1)S(1)} %pad_maximum_fusion.e_ref, bf16[64,512]{1,0:T(8,128)(2,1)S(1)} %collective-permute-done.2.top_ref, ...), custom_call_target="tpu_custom_call" | custom-call | flops 10000000000 | bytes 8000000 | tf_op jit(solution)/shard_map/columns/pallas_call | solution.py:160
  66.8 1.1 %copy-done.10 = bf16[32,64,384]{2,1,0:T(8,128)(2,1)} copy-done((bf16[32,64,384]{2,1,0:T(8,128)(2,1)}, bf16[32,64,384]{2,1,0:T(8,128)(2,1)S(1)}, u32[]{:S(2)}) %copy-start.10) | copy-done | bytes 1572888
  68.0 11.2 %all-to-all-start = ((bf16[64,64,128]{2,1,0:T(8,128)(2,1)}), bf16[64,64,128]{2,1,0:T(8,128)(2,1)}, u32[]{:S(2)}, u32[]{:S(2)}) async-start(bf16[64,64,128]{2,1,0:T(8,128)(2,1)} %get-tuple-element.7), calls=%async_computation | async-start | bytes 2097152 | tf_op jit(solution)/shard_map/all_to_all | solution.py:186
  79.1 0.0 copy-start.11
  79.1 1.4 %copy-done.11 = bf16[32,64,384]{2,1,0:T(8,128)(2,1)S(1)} copy-done((bf16[32,64,384]{2,1,0:T(8,128)(2,1)S(1)}, bf16[32,64,384]{2,1,0:T(8,128)(2,1)}, u32[]{:S(2)}) %copy-start.11) | copy-done | bytes 1572888
  80.5 14.8 %place.1 = bf16[32,64,384]{2,1,0:T(8,128)(2,1)S(1)} custom-call(s32[8192]{0:T(1024)S(1)} %bitcast.31, bf16[32,64,384]{2,1,0:T(8,128)(2,1)S(1)} %copy-done.11, bf16[8192,128]{1,0:T(8,128)(2,1)S(1)} %copy-done.9), custom_call_target="tpu_custom_call" | custom-call | flops 5000000000 | bytes 8000000 | tf_op jit(solution)/shard_map/place/pallas_call | solution.py:187
  95.4 2.1 %copy.23 = bf16[64,32,384]{2,1,0:T(8,128)(2,1)} copy(bf16[64,32,384]{2,0,1:T(8,128)(2,1)S(1)} %bitcast.28) | data formatting | bytes 3145728
  97.4 0.0 all-to-all-done
  97.4 2.3 %copy.22 = bf16[64,32,2,128]{3,2,1,0:T(2,128)(2,1)S(1)} copy(bf16[64,32,2,128]{3,0,2,1:T(8,128)(2,1)} %bitcast.16) | data formatting | bytes 2097152 | tf_op jit(solution)/shard_map/transpose | solution.py:204
  99.7 1.5 %reshape.39 = bf16[64,1,1,32,256]{4,3,2,1,0:T(8,128)(2,1)} reshape(bf16[64,32,2,128]{3,2,1,0:T(2,128)(2,1)S(1)} %copy.22) | data formatting | bytes 2097152 | tf_op jit(solution)/shard_map/reshape | solution.py:204
  (9 shorter events, 0.0 us)
Async XLA Ops:
  2.6 9.8 %copy-start.12 = (bf16[64,32,384]{2,0,1:T(8,128)(2,1)}, bf16[64,32,384]{2,0,1:T(8,128)(2,1)S(1)}, u32[]{:S(2)}) copy-start(bf16[64,32,384]{2,0,1:T(8,128)(2,1)S(1)} %copy.28) | copy-start | bytes 4718596
  2.9 14.8 %copy-start.14 = (bf16[9,64,64]{2,1,0:T(8,128)(2,1)S(1)}, bf16[9,64,64]{2,1,0:T(8,128)(2,1)}, u32[]{:S(2)}) copy-start(bf16[9,64,64]{2,1,0:T(8,128)(2,1)} %param.17) | copy-start | bytes 221188
  2.9 15.1 %copy-start.13 = (bf16[64,32,384]{2,1,0:T(8,128)(2,1)S(1)}, bf16[64,32,384]{2,1,0:T(8,128)(2,1)}, u32[]{:S(2)}) copy-start(bf16[64,32,384]{2,1,0:T(8,128)(2,1)} %param.16) | copy-start | bytes 4718596
  2.9 9.1 %collective-permute-start = (bf16[32,64,1]{2,1,0:T(8,128)(2,1)S(1)}, bf16[32,64,1]{2,1,0:T(8,128)(2,1)S(1)}, u32[]{:S(2)}, u32[]{:S(2)}) collective-permute-start(bf16[32,64,1]{2,1,0:T(8,128)(2,1)S(1)} %get-tuple-element.14), channel_id=1, source_target_pairs={{0,31},{1,0},{2,1},{3,2},{4,3},{5,4},{6,5},{7,6},{8,7},{9,8},{10,9... | collective-permute-start | bytes 12296 | tf_op jit(solution)/shard_map/ppermute | solution.py:135
  3.6 8.4 %collective-permute-start.1 = (bf16[32,64,1]{2,1,0:T(8,128)(2,1)S(1)}, bf16[32,64,1]{2,1,0:T(8,128)(2,1)S(1)}, u32[]{:S(2)}, u32[]{:S(2)}) collective-permute-start(bf16[32,64,1]{2,1,0:T(8,128)(2,1)S(1)} %get-tuple-element.15), channel_id=1, source_target_pairs={{0,1},{1,2},{2,3},{3,4},{4,5},{5,6},{6,7},{7,8},{8,9},{9,10},{10,1... | collective-permute-start | bytes 12296 | tf_op jit(solution)/shard_map/ppermute | solution.py:135
  12.4 7.4 %collective-permute-start.2 = (bf16[64,512]{1,0:T(8,128)(2,1)S(1)}, bf16[64,512]{1,0:T(8,128)(2,1)S(1)}, u32[]{:S(2)}, u32[]{:S(2)}) collective-permute-start(bf16[64,512]{1,0:T(8,128)(2,1)S(1)} %pad_maximum_fusion.1), channel_id=1, source_target_pairs={{0,32},{32,64},{64,96},{1,33},{33,65},{65,97},{2,34},{34,66},{66,9... | collective-permute-start | bytes 196616 | tf_op jit(solution)/shard_map/ppermute | solution.py:135
  15.6 5.2 %collective-permute-start.3 = (bf16[64,512]{1,0:T(8,128)(2,1)S(1)}, bf16[64,512]{1,0:T(8,128)(2,1)S(1)}, u32[]{:S(2)}, u32[]{:S(2)}) collective-permute-start(bf16[64,512]{1,0:T(8,128)(2,1)S(1)} %pad_maximum_fusion.2), channel_id=1, source_target_pairs={{32,0},{64,32},{96,64},{33,1},{65,33},{97,65},{34,2},{66,34},{98,6... | collective-permute-start | bytes 196616 | tf_op jit(solution)/shard_map/ppermute | solution.py:135
  18.0 2.8 %copy-start = (bf16[512,512]{1,0:T(8,128)(2,1)S(1)}, bf16[512,512]{1,0:T(8,128)(2,1)}, u32[]{:S(2)}) copy-start(bf16[512,512]{1,0:T(8,128)(2,1)} %w2_ref.1) | copy-start | bytes 1572868
  18.0 2.8 %copy-start.1 = (bf16[512,512]{1,0:T(8,128)(2,1)S(1)}, bf16[512,512]{1,0:T(8,128)(2,1)}, u32[]{:S(2)}) copy-start(bf16[512,512]{1,0:T(8,128)(2,1)} %w3_ref.1) | copy-start | bytes 1572868
  18.1 2.8 %copy-start.2 = (bf16[128,512]{1,0:T(8,128)(2,1)S(1)}, bf16[128,512]{1,0:T(8,128)(2,1)}, u32[]{:S(2)}) copy-start(bf16[128,512]{1,0:T(8,128)(2,1)} %w1_ref.1) | copy-start | bytes 393220
  18.1 2.8 %copy-start.3 = (bf16[512,128]{1,0:T(8,128)(2,1)S(1)}, bf16[512,128]{1,0:T(8,128)(2,1)}, u32[]{:S(2)}) copy-start(bf16[512,128]{1,0:T(8,128)(2,1)} %w4_ref.1) | copy-start | bytes 393220
  18.1 2.8 %copy-start.4 = (s32[1,1,8192]{2,1,0:T(1,128)S(1)}, s32[1,1,8192]{2,1,0:T(1,128)}, u32[]{:S(2)}) copy-start(s32[1,1,8192]{2,1,0:T(1,128)} %param.26) | copy-start | bytes 98308
  18.1 2.8 %copy-start.5 = (f32[512]{0:T(512)S(1)}, f32[512]{0:T(512)}, u32[]{:S(2)}) copy-start(f32[512]{0:T(512)} %param.19) | copy-start | bytes 6148
  18.1 2.8 %copy-start.6 = (f32[512]{0:T(512)S(1)}, f32[512]{0:T(512)}, u32[]{:S(2)}) copy-start(f32[512]{0:T(512)} %param.21) | copy-start | bytes 6148
  18.1 2.8 %copy-start.7 = (f32[512]{0:T(512)S(1)}, f32[512]{0:T(512)}, u32[]{:S(2)}) copy-start(f32[512]{0:T(512)} %param.23) | copy-start | bytes 6148
  18.1 2.8 %copy-start.8 = (f32[128]{0:T(128)S(1)}, f32[128]{0:T(128)}, u32[]{:S(2)}) copy-start(f32[128]{0:T(128)} %param.25) | copy-start | bytes 1540
  66.8 1.1 %copy-start.10 = (bf16[32,64,384]{2,1,0:T(8,128)(2,1)}, bf16[32,64,384]{2,1,0:T(8,128)(2,1)S(1)}, u32[]{:S(2)}) copy-start(bf16[32,64,384]{2,1,0:T(8,128)(2,1)S(1)} %get-tuple-element.5.dyn_ref) | copy-start | bytes 4718596
  68.0 11.2 %copy-start.9 = (bf16[8192,128]{1,0:T(8,128)(2,1)S(1)}, bf16[8192,128]{1,0:T(8,128)(2,1)}, u32[]{:S(2)}) copy-start(bf16[8192,128]{1,0:T(8,128)(2,1)} %get-tuple-element.6.tend_ref) | copy-start | bytes 6291460
  68.0 29.5 %all-to-all-start = ((bf16[64,64,128]{2,1,0:T(8,128)(2,1)}), bf16[64,64,128]{2,1,0:T(8,128)(2,1)}, u32[]{:S(2)}, u32[]{:S(2)}) async-start(bf16[64,64,128]{2,1,0:T(8,128)(2,1)} %get-tuple-element.7), calls=%async_computation | async-start | bytes 2097152 | tf_op jit(solution)/shard_map/all_to_all | solution.py:186
  79.1 1.4 %copy-start.11 = (bf16[32,64,384]{2,1,0:T(8,128)(2,1)S(1)}, bf16[32,64,384]{2,1,0:T(8,128)(2,1)}, u32[]{:S(2)}) copy-start(bf16[32,64,384]{2,1,0:T(8,128)(2,1)} %copy-done.10) | copy-start | bytes 4718596

commit v2 on v1

v2 whole, which is shorter than its diff:
```python
import jax
import jax.numpy as jnp
from jax import lax
from jax.experimental import pallas as pl
from jax.experimental.pallas import tpu as pltpu
from jax.sharding import PartitionSpec as P

K0 = 0.7978845608028654
K1 = K0 * 0.044715
LANES = 128
GROUP = 512
BF = jnp.bfloat16
F32 = jnp.float32


def lane_index(rows):
    return lax.broadcasted_iota(jnp.int32, (rows, LANES), 1)


def half_gelu(y):
    t = jnp.tanh(y * (2.0 * K0 + (8.0 * K1) * (y * y)))
    return (y + y * t).astype(BF)


def edges_kernel(low_ref, high_ref, pay_ref):
    chans, rows, _ = low_ref.shape
    lane = lane_index(rows)
    acc = jnp.zeros((rows, LANES), F32)
    for c in range(chans):
        low = jnp.broadcast_to(low_ref[c].astype(F32)[:, :1], (rows, LANES))
        high = jnp.broadcast_to(high_ref[c].astype(F32)[:, LANES - 1 :], (rows, LANES))
        acc = jnp.where(lane == c, low, jnp.where(lane == chans + c, high, acc))
    pay_ref[...] = acc.astype(BF)


def halo_columns(left_ref, right_ref, chans):
    rows = left_ref.shape[0]
    pad = jnp.zeros((LANES - rows, LANES), F32)
    left = jnp.concatenate([left_ref[...].astype(F32), pad], axis=0).T[chans : 2 * chans]
    right = jnp.concatenate([right_ref[...].astype(F32), pad], axis=0).T[:chans]
    return left, right


def halo_tile(left, right, y, chans):
    lane = lane_index(chans)
    low = jnp.broadcast_to(right[:, y : y + 1], (chans, LANES))
    high = jnp.broadcast_to(left[:, y : y + 1], (chans, LANES))
    return jnp.where(lane == 0, low, jnp.where(lane == LANES - 1, high, 0.0)).astype(BF)


def rows_kernel(left_ref, right_ref, first_ref, last_ref, up_ref, down_ref):
    _, chans, cols = first_ref.shape
    rows = left_ref.shape[0]
    left, right = halo_columns(left_ref, right_ref, chans)
    up_ref[:, :cols] = first_ref[0]
    up_ref[:, cols:] = halo_tile(left, right, 0, chans)
    down_ref[:, :cols] = last_ref[0]
    down_ref[:, cols:] = halo_tile(left, right, rows - 1, chans)


def columns_kernel(
    src, s_ref, left_ref, right_ref, top_ref, bot_ref, f_ref, cw_ref, w1_ref, b1_ref, w2_ref,
    b2_ref, w3_ref, b3_ref, w4_ref, b4_ref, vsrc_ref,
    dyn_ref, tend_ref, send_ref,
    ext, feats, buf0, buf1, w1h, w2h, w3h,
):
    rows, chans, cols = s_ref.shape
    cells = rows * cols
    owners, _, cap = send_ref.shape
    slots = tend_ref.shape[0]
    wide = cols + LANES
    groups = slots // GROUP
    ext[0] = top_ref[...]
    ext[rows + 1] = bot_ref[...]
    ext[1 : rows + 1, :, :cols] = s_ref[...]
    left, right = halo_columns(left_ref, right_ref, chans)
    for y in range(rows):
        ext[y + 1, :, cols:] = halo_tile(left, right, y, chans)
    feats[cells : cells + 8, :] = jnp.zeros((8, 2 * chans), F32)

    hid = w2h.shape[0]
    half = b1_ref[...] * 0.5
    high = half.astype(BF)
    rest = half - high.astype(F32)
    mid = rest.astype(BF)
    low = (rest - mid.astype(F32)).astype(BF)
    row = lax.broadcasted_iota(jnp.int32, (LANES, hid), 0)
    w1h[:LANES] = w1_ref[...] * BF(0.5)
    w1h[LANES:] = jnp.where(
        row == 0, high.astype(F32), jnp.where(row == 1, mid.astype(F32), jnp.where(row == 2, low.astype(F32), 0.0))
    ).astype(BF)
    w2h[...] = w2_ref[...] * BF(0.5)
    w3h[...] = w3_ref[...] * BF(0.5)

    def conv_row(y, carry):
        x = ext[pl.ds(y, 3)].reshape(3 * chans, wide)
        p = jnp.dot(cw_ref[...], x, preferred_element_type=F32)
        total = (
            s_ref[y].astype(F32)
            + p[chans : 2 * chans, :cols]
            + pltpu.roll(p[:chans], 1, 1)[:, :cols]
            + pltpu.roll(p[2 * chans :], wide - 1, 1)[:, :cols]
        )
        dyn = total.astype(BF)
        dyn_ref[y] = dyn
        both = jnp.concatenate([dyn.astype(F32), f_ref[y].astype(F32)], axis=0)
        feats[pl.ds(pl.multiple_of(y * cols, LANES), cols), :] = both.T
        return carry

    lax.fori_loop(0, rows, conv_row, 0, unroll=8)

    def fetch(g, buf, start, stop):
        base = jnp.minimum(g, groups - 1) * GROUP
        for r in range(start, stop):
            buf[pl.ds(r, 1), :] = feats[pl.ds(src[base + r], 1), :]

    ones = jnp.ones((GROUP, LANES), BF)

    def net(g, buf, following):
        part = GROUP // 4
        h = jnp.concatenate([buf[...].astype(BF), ones], axis=1)
        fetch(g + 1, following, 0, part)
        h = half_gelu(jnp.dot(h, w1h[...], preferred_element_type=F32))
        fetch(g + 1, following, part, 2 * part)
        h = half_gelu(jnp.dot(h, w2h[...], preferred_element_type=F32) + b2_ref[...] * 0.5)
        fetch(g + 1, following, 2 * part, 3 * part)
        h = half_gelu(jnp.dot(h, w3h[...], preferred_element_type=F32) + b3_ref[...] * 0.5)
        fetch(g + 1, following, 3 * part, GROUP)
        out = jnp.dot(h, w4_ref[...], preferred_element_type=F32) + b4_ref[...]
        tend_ref[pl.ds(pl.multiple_of(g * GROUP, GROUP), GROUP), :] = out.astype(BF)
        flip = out.T[chans:]
        for j in range(GROUP // cap):
            o = g * (GROUP // cap) + j
            diag = jnp.where(vsrc_ref[pl.ds(o, 1), :] < cells, flip[:, j * cap : (j + 1) * cap], 0.0)
            send_ref[o] = diag.astype(BF)

    fetch(0, buf0, 0, GROUP)

    def pair(i, carry):
        net(2 * i, buf0, buf1)
        net(2 * i + 1, buf1, buf0)
        return carry

    lax.fori_loop(0, groups // 2, pair, 0)


def place_kernel(src, dyn_ref, tend_ref, new_ref, acc, rows_f32):
    rows, chans, cols = dyn_ref.shape
    slots = tend_ref.shape[0]

    acc[...] = jnp.zeros(acc.shape, F32)

    def block(n, carry):
        base = n * LANES
        rows_f32[...] = tend_ref[pl.ds(pl.multiple_of(base, LANES), LANES), :].astype(F32)
        for r in range(LANES):
            acc[pl.ds(src[base + r], 1), :] = rows_f32[pl.ds(r, 1), :]
        return carry

    lax.fori_loop(0, slots // LANES, block, 0)

    def row(y, carry):
        part = acc[pl.ds(pl.multiple_of(y * cols, LANES), cols), :].T[:chans]
        new_ref[y] = (dyn_ref[y].astype(F32) + part).astype(BF)
        return carry

    lax.fori_loop(0, rows, row, 0, unroll=4)


def owned_kernel(got_ref, out_ref, wide):
    owners, chans, cap = got_ref.shape
    for h in range(cap // LANES):
        part = slice(h * LANES, (h + 1) * LANES)
        for s in range(owners):
            wide[h, pl.ds(s, chans, stride=owners), :] = got_ref[s, :, part].astype(F32)
        for c in range(chans):
            out_ref[c, :, part] = wide[h, c * owners : (c + 1) * owners, :].astype(BF)


def shift(block, axis, step, periodic):
    count = lax.axis_size(axis)
    pairs = [(i, (i + step) % count) for i in range(count) if periodic or 0 <= i + step < count]
    return lax.ppermute(block, axis, pairs)


def body(
    state, forcing, conv_weight, w_first, b_first, w_second, b_second, w_third, b_third,
    w_final, b_final, active, owner, slot, source,
):
    chans, rows, cols = state.shape
    slots = source.size
    cells = rows * cols
    hid = w_second.shape[0]
    owners = lax.axis_size("lon")
    cap = slots // owners
    wide = cols + LANES
    src = source.reshape(slots)
    vmem = pl.BlockSpec(memory_space=pltpu.VMEM)
    smem = pl.BlockSpec(memory_space=pltpu.SMEM)

    tile = (chans, rows, LANES)
    pay = pl.pallas_call(
        edges_kernel,
        grid=(1,),
        out_shape=jax.ShapeDtypeStruct((rows, LANES), BF),
        in_specs=[
            pl.BlockSpec(tile, lambda i: (0, 0, 0)),
            pl.BlockSpec(tile, lambda i: (0, 0, cols // LANES - 1)),
        ],
        out_specs=pl.BlockSpec((rows, LANES), lambda i: (0, 0)),
        name="edges",
    )(state, state)
    left = shift(pay, "lon", 1, True)
    right = shift(pay, "lon", -1, True)
    s = state.transpose(1, 0, 2)
    f = forcing.transpose(1, 0, 2)
    cw = conv_weight.reshape(3, 3, chans, chans).transpose(1, 2, 0, 3).reshape(3 * chans, 3 * chans)
    whole = pl.BlockSpec((rows, LANES), lambda i: (0, 0))
    up, down = pl.pallas_call(
        rows_kernel,
        grid=(1,),
        out_shape=(jax.ShapeDtypeStruct((chans, wide), BF),) * 2,
        in_specs=[
            whole,
            whole,
            pl.BlockSpec((1, chans, cols), lambda i: (0, 0, 0)),
            pl.BlockSpec((1, chans, cols), lambda i: (rows - 1, 0, 0)),
        ],
        out_specs=(pl.BlockSpec((chans, wide), lambda i: (0, 0)),) * 2,
        name="rows",
    )(left, right, s, s)
    top = shift(down, "lat", 1, False)
    bot = shift(up, "lat", -1, False)

    dyn, tend, send = pl.pallas_call(
        columns_kernel,
        out_shape=(
            jax.ShapeDtypeStruct((rows, chans, cols), BF),
            jax.ShapeDtypeStruct((slots, 2 * chans), BF),
            jax.ShapeDtypeStruct((owners, chans, cap), BF),
        ),
        in_specs=[smem] + [vmem] * 16,
        out_specs=(vmem, vmem, vmem),
        scratch_shapes=[
            pltpu.VMEM((rows + 2, chans, wide), BF),
            pltpu.VMEM((cells + 8, 2 * chans), F32),
            pltpu.VMEM((GROUP, 2 * chans), F32),
            pltpu.VMEM((GROUP, 2 * chans), F32),
            pltpu.VMEM((2 * LANES, hid), BF),
            pltpu.VMEM(w_second.shape, BF),
            pltpu.VMEM(w_third.shape, BF),
        ],
        compiler_params=pltpu.CompilerParams(vmem_limit_bytes=40 << 20),
        cost_estimate=pl.CostEstimate(flops=10_000_000_000, bytes_accessed=8_000_000, transcendentals=12_000_000),
        name="columns",
    )(
        src, s, left, right, top, bot, f, cw, w_first, b_first.reshape(1, hid), w_second,
        b_second.reshape(1, hid), w_third, b_third.reshape(1, hid), w_final,
        b_final.reshape(1, 2 * chans), src.reshape(owners, cap),
    )
    got = lax.all_to_all(send, "lon", split_axis=0, concat_axis=0, tiled=True)
    new = pl.pallas_call(
        place_kernel,
        out_shape=jax.ShapeDtypeStruct((rows, chans, cols), BF),
        in_specs=[smem, vmem, vmem],
        out_specs=vmem,
        scratch_shapes=[
            pltpu.VMEM((cells + 8, 2 * chans), F32),
            pltpu.VMEM((LANES, 2 * chans), F32),
        ],
        compiler_params=pltpu.CompilerParams(vmem_limit_bytes=32 << 20),
        cost_estimate=pl.CostEstimate(flops=5_000_000_000, bytes_accessed=8_000_000, transcendentals=0),
        name="place",
    )(src, dyn, tend)
    new_state = new.transpose(1, 0, 2)
    owned = pl.pallas_call(
        owned_kernel,
        out_shape=jax.ShapeDtypeStruct((chans, owners, cap), BF),
        in_specs=[vmem],
        out_specs=vmem,
        scratch_shapes=[pltpu.VMEM((cap // LANES, chans * owners, LANES), F32)],
        compiler_params=pltpu.CompilerParams(vmem_limit_bytes=16 << 20),
        name="owned",
    )(got)
    return (new_state, owned.reshape(chans, 1, 1, owners, cap))


def solution(mesh):
    field = P(None, "lat", "lon")
    return jax.shard_map(
        body,
        mesh=mesh,
        in_specs=(field, field) + (P(),) * 9 + (P("lat", "lon"),) * 3 + (P("lat", "lon", None),),
        out_specs=(field, P(None, "lat", "lon", None, None)),
        check_vma=False,
    )
```

time: 103 us -> 81.9 us (0.80)
  Pallas kernels: 60.7 us -> 45.3 us
  local copies, waits for them, and re-layouts: 12.8 us -> 8.53 us
    pallas_call x1, Pallas kernels: 45.9 us -> 27.6 us  [body(): pl.pallas_call(columns_kernel, out_shape=(jax.ShapeDtypeStruct((rows, cha...]
    pallas_call x0 -> x3, Pallas kernels: none -> 7.36 us  [the longest x1 3.16 us: body(): pl.pallas_call(owned_kernel, out_shape=jax.ShapeDtypeStruct((chans, owner...]
    pallas_call x1, Pallas kernels: 14.8 us -> 10.4 us  [body(): pl.pallas_call(place_kernel, out_shape=jax.ShapeDtypeStruct((rows, chans,...]
    ppermute x4, waiting for transfers between devices: 7.7 us -> 4.21 us  [shift(): return lax.ppermute(block, axis, pairs)]
    all_to_all x1, waiting for transfers between devices: 0.01 us -> 3.14 us  [body(): got = lax.all_to_all(send, 'lon', split_axis=0, concat_axis=0, tiled=True)]
    transpose x1 -> x0, local copies, waits for them, and re-layouts: 2.3 us -> none  [body(): got.reshape(owners, halves, chans, SUB).transpose(2, 0, 1, 3)]
    reshape x1 -> x0, local copies, waits for them, and re-layouts: 1.49 us -> none  [body(): got.reshape(owners, halves, chans, SUB).transpose(2, 0, 1, 3)]
    unnamed x33 -> x42, local copies, waits for them, and re-layouts: 8.32 us -> 8.23 us
  transfers between devices with their start and end apart: 5 -> 5, of which waited for: 2 -> 3; matrix products, arithmetic and copies ran while one was open for 4% -> 7% of each run, Pallas kernels for 15% -> 13%
where the time goes in v2:
time: 81.9 us; the launch traced here: 80.8 us
  Pallas kernels  45.3 us (55%)
  starting transfers between devices  18.1 us (22%)
  local copies, waits for them, and re-layouts  8.53 us (10%)
  waiting for transfers between devices  7.35 us (9%)
  between operations  0.84 us (1%)
    pallas_call x1, Pallas kernels, body(): pl.pallas_call(columns_kernel, out_shape=(jax.ShapeDtypeStruct((rows, cha...  27.6 us
    all_to_all x1, starting transfers between devices, body(): got = lax.all_to_all(send, 'lon', split_axis=0, concat_axis=0, tiled=True)  10.6 us
    pallas_call x1, Pallas kernels, body(): pl.pallas_call(place_kernel, out_shape=jax.ShapeDtypeStruct((rows, chans,...  10.4 us
    unnamed x42, local copies, waits for them, and re-layouts  8.23 us
    ppermute x4, starting transfers between devices, shift(): return lax.ppermute(block, axis, pairs)  7.47 us
    ppermute x4, waiting for transfers between devices, shift(): return lax.ppermute(block, axis, pairs)  4.21 us
    pallas_call x1, Pallas kernels, body(): pl.pallas_call(owned_kernel, out_shape=jax.ShapeDtypeStruct((chans, owner...  3.16 us
    all_to_all x1, waiting for transfers between devices, body(): got = lax.all_to_all(send, 'lon', split_axis=0, concat_axis=0, tiled=True)  3.14 us
  transfers between devices with their start and end apart: 5, of which 3 were waited for; matrix products, arithmetic and copies ran while one was open for 7% of the time, Pallas kernels for 13%

profile of v2, /device:TPU:9, one launch (start us, length us, event | category | flops | bytes accessed | tf_op | source)
XLA Modules:
  0.0 80.8 jit_solution(2696034772055731378)
XLA Ops:
  0.6 0.0 copy-start.16
  0.6 2.4 %edges.1 = bf16[32,128]{1,0:T(8,128)(2,1)} custom-call(bf16[64,32,384]{2,1,0:T(8,128)(2,1)} %high_ref.1, bf16[64,32,384]{2,1,0:T(8,128)(2,1)} %high_ref.1), custom_call_target="tpu_custom_call" | custom-call | tf_op jit(solution)/shard_map/edges/pallas_call | solution.py:202
  3.0 0.7 collective-permute-start.1
  3.7 1.5 %collective-permute-start = (bf16[32,128]{1,0:T(8,128)(2,1)}, bf16[32,128]{1,0:T(8,128)(2,1)S(1)}, u32[]{:S(2)}, u32[]{:S(2)}) collective-permute-start(bf16[32,128]{1,0:T(8,128)(2,1)} %edges.1), channel_id=1, source_target_pairs={{0,1},{1,2},{2,3},{3,4},{4,5},{5,6},{6,7},{7,8},{8,9},{9,10},{10,1... | collective-permute-start | bytes 24584 | tf_op jit(solution)/shard_map/ppermute | solution.py:183
  5.2 0.0 copy-done.16
  5.2 1.7 %copy.28 = bf16[64,32,384]{2,0,1:T(8,128)(2,1)} copy(bf16[64,32,384]{2,1,0:T(8,128)(2,1)S(1)} %copy-done.16) | data formatting | bytes 3145728 | tf_op args[0]
  6.9 0.0 collective-permute-done.1.right_ref
  6.9 3.3 %collective-permute-done.left_ref = bf16[32,128]{1,0:T(8,128)(2,1)S(1)} collective-permute-done((bf16[32,128]{1,0:T(8,128)(2,1)}, bf16[32,128]{1,0:T(8,128)(2,1)S(1)}, u32[]{:S(2)}, u32[]{:S(2)}) %collective-permute-start) | collective-permute-done | bytes 8224 | tf_op jit(solution)/shard_map/ppermute | solution.py:183
  10.3 0.0 copy-done.2
  10.3 0.6 copy-done.4
  10.9 1.8 %rows.1 = (bf16[64,512]{1,0:T(8,128)(2,1)}, bf16[64,512]{1,0:T(8,128)(2,1)}) custom-call(bf16[32,128]{1,0:T(8,128)(2,1)} %copy-done.4, bf16[32,128]{1,0:T(8,128)(2,1)} %copy-done.2, bf16[32,64,384]{2,1,0:T(8,128)(2,1)} %bitcast.19, bf16[32,64,384]{2,1,0:T(8,128)(2,1)} %bitcast.20), custom_call_target="tpu_custom_call" | custom-call | tf_op jit(solution)/shard_map/rows/pallas_call | solution.py:219
  12.7 3.2 %collective-permute-start.2 = (bf16[64,512]{1,0:T(8,128)(2,1)}, bf16[64,512]{1,0:T(8,128)(2,1)S(1)}, u32[]{:S(2)}, u32[]{:S(2)}) collective-permute-start(bf16[64,512]{1,0:T(8,128)(2,1)} %get-tuple-element.7), channel_id=1, source_target_pairs={{0,32},{32,64},{64,96},{1,33},{33,65},{65,97},{2,34},{34,66},{66,9... | collective-permute-start | bytes 196616 | tf_op jit(solution)/shard_map/ppermute | solution.py:183
  15.9 2.1 %collective-permute-start.3 = (bf16[64,512]{1,0:T(8,128)(2,1)}, bf16[64,512]{1,0:T(8,128)(2,1)S(1)}, u32[]{:S(2)}, u32[]{:S(2)}) collective-permute-start(bf16[64,512]{1,0:T(8,128)(2,1)} %get-tuple-element.8), channel_id=1, source_target_pairs={{32,0},{64,32},{96,64},{33,1},{65,33},{97,65},{34,2},{66,34},{98,6... | collective-permute-start | bytes 196616 | tf_op jit(solution)/shard_map/ppermute | solution.py:183
  17.9 0.5 broadcast.3
  18.5 0.0 copy-done.1
  18.5 0.7 reduce.3
  19.2 0.0 copy-done.18
  19.2 0.1 copy.29
  19.3 0.2 reshape.30.cw_ref
  19.5 0.0 copy-done.17
  19.5 0.0 copy-start
  19.5 0.0 copy-start.3
  19.5 0.0 copy-start.6
  19.6 0.0 copy-start.7
  19.6 0.0 copy-start.8
  19.6 0.0 copy-start.9
  19.6 0.0 copy-start.10
  19.6 0.0 copy-start.11
  19.6 0.0 copy-start.12
  19.6 0.0 copy-start.13
  19.6 0.5 copy.27
  20.2 0.0 collective-permute-done.2.top_ref
  20.2 0.9 %collective-permute-done.3.bot_ref = bf16[64,512]{1,0:T(8,128)(2,1)S(1)} collective-permute-done((bf16[64,512]{1,0:T(8,128)(2,1)}, bf16[64,512]{1,0:T(8,128)(2,1)S(1)}, u32[]{:S(2)}, u32[]{:S(2)}) %collective-permute-start.3) | collective-permute-done | bytes 65568 | tf_op jit(solution)/shard_map/ppermute | solution.py:183
  21.1 0.0 copy-done
  21.1 0.1 copy-done.7
  21.2 0.0 copy-done.8
  21.2 0.0 copy-done.9
  21.3 0.0 copy-done.10
  21.3 0.0 copy-done.12
  21.3 27.6 %columns.1 = (bf16[32,64,384]{2,1,0:T(8,128)(2,1)S(1)}, bf16[8192,128]{1,0:T(8,128)(2,1)S(1)}, bf16[32,64,256]{2,1,0:T(8,128)(2,1)}) custom-call(s32[8192]{0:T(1024)S(1)} %bitcast.24, bf16[32,64,384]{2,1,0:T(8,128)(2,1)S(1)} %bitcast.21, bf16[32,128]{1,0:T(8,128)(2,1)S(1)} %copy-done.5, bf16[32,128]{1,0:T(8,128)(2,1)S(1)} %copy-done.3, ...), custom_call_target="tpu_custom_call" | custom-call | flops 10000000000 | bytes 8000000 | tf_op jit(solution)/shard_map/columns/pallas_call | solution.py:235
  48.9 1.1 %copy-done.14 = bf16[32,64,384]{2,1,0:T(8,128)(2,1)} copy-done((bf16[32,64,384]{2,1,0:T(8,128)(2,1)}, bf16[32,64,384]{2,1,0:T(8,128)(2,1)S(1)}, u32[]{:S(2)}) %copy-start.14) | copy-done | bytes 1572888
  50.0 10.6 %all-to-all-start = ((bf16[32,64,256]{2,1,0:T(8,128)(2,1)}), bf16[32,64,256]{2,1,0:T(8,128)(2,1)S(1)}, u32[]{:S(2)}, u32[]{:S(2)}) async-start(bf16[32,64,256]{2,1,0:T(8,128)(2,1)} %get-tuple-element.11), calls=%async_computation | async-start | bytes 2097152 | tf_op jit(solution)/shard_map/all_to_all | solution.py:261
  60.7 0.0 copy-start.15
  60.7 1.4 %copy-done.15 = bf16[32,64,384]{2,1,0:T(8,128)(2,1)S(1)} copy-done((bf16[32,64,384]{2,1,0:T(8,128)(2,1)S(1)}, bf16[32,64,384]{2,1,0:T(8,128)(2,1)}, u32[]{:S(2)}) %copy-start.15) | copy-done | bytes 1572888
  62.1 10.4 %place.1 = bf16[32,64,384]{2,1,0:T(8,128)(2,1)S(1)} custom-call(s32[8192]{0:T(1024)S(1)} %bitcast.25, bf16[32,64,384]{2,1,0:T(8,128)(2,1)S(1)} %copy-done.15, bf16[8192,128]{1,0:T(8,128)(2,1)S(1)} %get-tuple-element.10.tend_ref), custom_call_target="tpu_custom_call" | custom-call | flops 5000000000 | bytes 8000000 | tf_op jit(solution)/shard_map/place/pallas_call | solution.py:262
  72.5 2.1 %copy.22 = bf16[64,32,384]{2,1,0:T(8,128)(2,1)} copy(bf16[64,32,384]{2,0,1:T(8,128)(2,1)S(1)} %bitcast.23) | data formatting | bytes 3145728
  74.5 3.1 %all-to-all-done.got_ref = bf16[32,64,256]{2,1,0:T(8,128)(2,1)S(1)} async-done(((bf16[32,64,256]{2,1,0:T(8,128)(2,1)}), bf16[32,64,256]{2,1,0:T(8,128)(2,1)S(1)}, u32[]{:S(2)}, u32[]{:S(2)}) %all-to-all-start) | async-done | bytes 1048608 | tf_op jit(solution)/shard_map/all_to_all | solution.py:261
  77.7 3.2 %owned.1 = bf16[64,32,256]{2,1,0:T(8,128)(2,1)} custom-call(bf16[32,64,256]{2,1,0:T(8,128)(2,1)S(1)} %all-to-all-done.got_ref), custom_call_target="tpu_custom_call" | custom-call | tf_op jit(solution)/shard_map/owned/pallas_call | solution.py:276
  (13 shorter events, 0.0 us)
Async XLA Ops:
  0.6 4.6 %copy-start.16 = (bf16[64,32,384]{2,1,0:T(8,128)(2,1)S(1)}, bf16[64,32,384]{2,1,0:T(8,128)(2,1)}, u32[]{:S(2)}) copy-start(bf16[64,32,384]{2,1,0:T(8,128)(2,1)} %high_ref.1) | copy-start | bytes 4718596
  3.0 3.9 %collective-permute-start.1 = (bf16[32,128]{1,0:T(8,128)(2,1)}, bf16[32,128]{1,0:T(8,128)(2,1)S(1)}, u32[]{:S(2)}, u32[]{:S(2)}) collective-permute-start(bf16[32,128]{1,0:T(8,128)(2,1)} %edges.1), channel_id=1, source_target_pairs={{0,31},{1,0},{2,1},{3,2},{4,3},{5,4},{6,5},{7,6},{8,7},{9,8},{10,9... | collective-permute-start | bytes 24584 | tf_op jit(solution)/shard_map/ppermute | solution.py:183
  3.7 6.5 %collective-permute-start = (bf16[32,128]{1,0:T(8,128)(2,1)}, bf16[32,128]{1,0:T(8,128)(2,1)S(1)}, u32[]{:S(2)}, u32[]{:S(2)}) collective-permute-start(bf16[32,128]{1,0:T(8,128)(2,1)} %edges.1), channel_id=1, source_target_pairs={{0,1},{1,2},{2,3},{3,4},{4,5},{5,6},{6,7},{7,8},{8,9},{9,10},{10,1... | collective-permute-start | bytes 24584 | tf_op jit(solution)/shard_map/ppermute | solution.py:183
  6.9 3.3 %copy-start.2 = (bf16[32,128]{1,0:T(8,128)(2,1)}, bf16[32,128]{1,0:T(8,128)(2,1)S(1)}, u32[]{:S(2)}) copy-start(bf16[32,128]{1,0:T(8,128)(2,1)S(1)} %collective-permute-done.1.right_ref) | copy-start | bytes 24580
  10.3 0.6 copy-start.4
  10.8 7.6 %copy-start.1 = (s32[1,1,8192]{2,1,0:T(1,128)S(1)}, s32[1,1,8192]{2,1,0:T(1,128)}, u32[]{:S(2)}) copy-start(s32[1,1,8192]{2,1,0:T(1,128)} %param.26) | copy-start | bytes 98308
  10.8 8.4 %copy-start.18 = (bf16[9,64,64]{2,1,0:T(8,128)(2,1)S(1)}, bf16[9,64,64]{2,1,0:T(8,128)(2,1)}, u32[]{:S(2)}) copy-start(bf16[9,64,64]{2,1,0:T(8,128)(2,1)} %param.17) | copy-start | bytes 221188
  10.9 8.7 %copy-start.17 = (bf16[64,32,384]{2,1,0:T(8,128)(2,1)S(1)}, bf16[64,32,384]{2,1,0:T(8,128)(2,1)}, u32[]{:S(2)}) copy-start(bf16[64,32,384]{2,1,0:T(8,128)(2,1)} %param.16) | copy-start | bytes 4718596
  12.7 7.5 %collective-permute-start.2 = (bf16[64,512]{1,0:T(8,128)(2,1)}, bf16[64,512]{1,0:T(8,128)(2,1)S(1)}, u32[]{:S(2)}, u32[]{:S(2)}) collective-permute-start(bf16[64,512]{1,0:T(8,128)(2,1)} %get-tuple-element.7), channel_id=1, source_target_pairs={{0,32},{32,64},{64,96},{1,33},{33,65},{65,97},{2,34},{34,66},{66,9... | collective-permute-start | bytes 196616 | tf_op jit(solution)/shard_map/ppermute | solution.py:183
  15.9 5.2 %collective-permute-start.3 = (bf16[64,512]{1,0:T(8,128)(2,1)}, bf16[64,512]{1,0:T(8,128)(2,1)S(1)}, u32[]{:S(2)}, u32[]{:S(2)}) collective-permute-start(bf16[64,512]{1,0:T(8,128)(2,1)} %get-tuple-element.8), channel_id=1, source_target_pairs={{32,0},{64,32},{96,64},{33,1},{65,33},{97,65},{34,2},{66,34},{98,6... | collective-permute-start | bytes 196616 | tf_op jit(solution)/shard_map/ppermute | solution.py:183
  19.5 1.6 %copy-start = (bf16[64,32,384]{2,0,1:T(8,128)(2,1)S(1)}, bf16[64,32,384]{2,0,1:T(8,128)(2,1)}, u32[]{:S(2)}) copy-start(bf16[64,32,384]{2,0,1:T(8,128)(2,1)} %copy.28) | copy-start | bytes 4718596
  19.5 1.6 %copy-start.3 = (bf16[32,128]{1,0:T(8,128)(2,1)S(1)}, bf16[32,128]{1,0:T(8,128)(2,1)}, u32[]{:S(2)}) copy-start(bf16[32,128]{1,0:T(8,128)(2,1)} %copy-done.2) | copy-start | bytes 24580
  19.5 1.5 %copy-start.5 = (bf16[32,128]{1,0:T(8,128)(2,1)S(1)}, bf16[32,128]{1,0:T(8,128)(2,1)}, u32[]{:S(2)}) copy-start(bf16[32,128]{1,0:T(8,128)(2,1)} %copy-done.4) | copy-start | bytes 24580
  19.5 1.5 %copy-start.6 = (bf16[512,512]{1,0:T(8,128)(2,1)S(1)}, bf16[512,512]{1,0:T(8,128)(2,1)}, u32[]{:S(2)}) copy-start(bf16[512,512]{1,0:T(8,128)(2,1)} %w2_ref.1) | copy-start | bytes 1572868
  19.6 1.7 %copy-start.7 = (bf16[512,512]{1,0:T(8,128)(2,1)S(1)}, bf16[512,512]{1,0:T(8,128)(2,1)}, u32[]{:S(2)}) copy-start(bf16[512,512]{1,0:T(8,128)(2,1)} %w3_ref.1) | copy-start | bytes 1572868
  19.6 1.7 %copy-start.8 = (bf16[128,512]{1,0:T(8,128)(2,1)S(1)}, bf16[128,512]{1,0:T(8,128)(2,1)}, u32[]{:S(2)}) copy-start(bf16[128,512]{1,0:T(8,128)(2,1)} %w1_ref.1) | copy-start | bytes 393220
  19.6 1.7 %copy-start.9 = (bf16[512,128]{1,0:T(8,128)(2,1)S(1)}, bf16[512,128]{1,0:T(8,128)(2,1)}, u32[]{:S(2)}) copy-start(bf16[512,128]{1,0:T(8,128)(2,1)} %w4_ref.1) | copy-start | bytes 393220
  19.6 1.7 %copy-start.10 = (f32[512]{0:T(512)S(1)}, f32[512]{0:T(512)}, u32[]{:S(2)}) copy-start(f32[512]{0:T(512)} %param.19) | copy-start | bytes 6148
  19.6 1.7 %copy-start.11 = (f32[512]{0:T(512)S(1)}, f32[512]{0:T(512)}, u32[]{:S(2)}) copy-start(f32[512]{0:T(512)} %param.21) | copy-start | bytes 6148
  19.6 1.7 %copy-start.12 = (f32[512]{0:T(512)S(1)}, f32[512]{0:T(512)}, u32[]{:S(2)}) copy-start(f32[512]{0:T(512)} %param.23) | copy-start | bytes 6148
  19.6 1.7 %copy-start.13 = (f32[128]{0:T(128)S(1)}, f32[128]{0:T(128)}, u32[]{:S(2)}) copy-start(f32[128]{0:T(128)} %param.25) | copy-start | bytes 1540
  48.9 1.1 %copy-start.14 = (bf16[32,64,384]{2,1,0:T(8,128)(2,1)}, bf16[32,64,384]{2,1,0:T(8,128)(2,1)S(1)}, u32[]{:S(2)}) copy-start(bf16[32,64,384]{2,1,0:T(8,128)(2,1)S(1)} %get-tuple-element.9.dyn_ref) | copy-start | bytes 4718596
  50.0 27.6 %all-to-all-start = ((bf16[32,64,256]{2,1,0:T(8,128)(2,1)}), bf16[32,64,256]{2,1,0:T(8,128)(2,1)S(1)}, u32[]{:S(2)}, u32[]{:S(2)}) async-start(bf16[32,64,256]{2,1,0:T(8,128)(2,1)} %get-tuple-element.11), calls=%async_computation | async-start | bytes 2097152 | tf_op jit(solution)/shard_map/all_to_all | solution.py:261
  60.7 1.4 %copy-start.15 = (bf16[32,64,384]{2,1,0:T(8,128)(2,1)S(1)}, bf16[32,64,384]{2,1,0:T(8,128)(2,1)}, u32[]{:S(2)}) copy-start(bf16[32,64,384]{2,1,0:T(8,128)(2,1)} %copy-done.14) | copy-start | bytes 4718596

commit v3 on v2

--- a/solution.py
+++ b/solution.py
@@ -9,6 +9,8 @@
 K1 = K0 * 0.044715
 LANES = 128
 GROUP = 512
+CHUNK = 8
+PITCH = 33
 BF = jnp.bfloat16
 F32 = jnp.float32
 
@@ -59,25 +61,82 @@
 
 
 def columns_kernel(
-    src, s_ref, left_ref, right_ref, top_ref, bot_ref, f_ref, cw_ref, w1_ref, b1_ref, w2_ref,
-    b2_ref, w3_ref, b3_ref, w4_ref, b4_ref, vsrc_ref,
-    dyn_ref, tend_ref, send_ref,
-    ext, feats, buf0, buf1, w1h, w2h, w3h,
+    src, s_any, left_ref, right_ref, top_ref, bot_ref, f_any, cw_ref,
+    w1_any, b1_ref, w2_any, b2_ref, w3_any, b3_ref, w4_any, b4_ref, vsrc_ref,
+    dyn_any, tend_ref, send_ref,
+    ext, feats, f_ref, dyn_ref, buf0, buf1, w1h, w2h, w3h, w1_ref, w2_ref, w3_ref, w4_ref,
+    tend_buf, send_buf, s_sems, f_sems, dyn_sems, w_sems, tend_sems, send_sems,
 ):
-    rows, chans, cols = s_ref.shape
+    rows, chans, cols = f_ref.shape
     cells = rows * cols
     owners, _, cap = send_ref.shape
     slots = tend_ref.shape[0]
+    groups = slots // GROUP
     wide = cols + LANES
-    groups = slots // GROUP
+    chunks = rows // CHUNK
+
+    def s_load(k):
+        at = k * CHUNK
+        target = ext.at[pl.ds(at + 1, CHUNK), :, pl.ds(0, cols)]
+        return pltpu.make_async_copy(s_any.at[pl.ds(at, CHUNK)], target, s_sems.at[k])
+
+    def f_load(k):
+        part = pl.ds(k * CHUNK, CHUNK)
+        return pltpu.make_async_copy(f_any.at[part], f_ref.at[part], f_sems.at[k])
+
+    def dyn_store(k):
+        part = pl.ds(k * CHUNK, CHUNK)
+        return pltpu.make_async_copy(dyn_ref.at[part], dyn_any.at[part], dyn_sems.at[k])
+
+    for k in range(chunks):
+        s_load(k).start()
+        f_load(k).start()
+    loads = [
+        pltpu.make_async_copy(source, target, w_sems.at[k])
+        for k, (source, target) in enumerate(
+            ((w1_any, w1_ref), (w2_any, w2_ref), (w3_any, w3_ref), (w4_any, w4_ref))
+        )
+    ]
+    for load in loads:
+        load.start()
     ext[0] = top_ref[...]
     ext[rows + 1] = bot_ref[...]
-    ext[1 : rows + 1, :, :cols] = s_ref[...]
     left, right = halo_columns(left_ref, right_ref, chans)
     for y in range(rows):
         ext[y + 1, :, cols:] = halo_tile(left, right, y, chans)
     feats[cells : cells + 8, :] = jnp.zeros((8, 2 * chans), F32)
 
+    def conv_row(y):
+        x = ext[pl.ds(y, 3)].reshape(3 * chans, wide)
+        p = jnp.dot(cw_ref[...], x, preferred_element_type=F32)
+        total = (
+            x[chans : 2 * chans, :cols].astype(F32)
+            + p[chans : 2 * chans, :cols]
+            + pltpu.roll(p[:chans], 1, 1)[:, :cols]
+            + pltpu.roll(p[2 * chans :], wide - 1, 1)[:, :cols]
+        )
+        dyn = total.astype(BF)
+        dyn_ref[y] = dyn
+        both = jnp.concatenate([dyn.astype(F32), f_ref[y].astype(F32)], axis=0)
+        feats[pl.ds(pl.multiple_of(y * cols, LANES), cols), :] = both.T
+
+    s_load(0).wait()
+
+    def chunk(k, carry):
+        @pl.when(k < chunks - 1)
+        def _():
+            s_load(jnp.minimum(k + 1, chunks - 1)).wait()
+
+        f_load(k).wait()
+        for n in range(CHUNK):
+            conv_row(k * CHUNK + n)
+        dyn_store(k).start()
+        return carry
+
+    lax.fori_loop(0, chunks, chunk, 0)
+
+    for load in loads:
+        load.wait()
     hid = w2h.shape[0]
     half = b1_ref[...] * 0.5
     high = half.astype(BF)
@@ -92,29 +151,26 @@
     w2h[...] = w2_ref[...] * BF(0.5)
     w3h[...] = w3_ref[...] * BF(0.5)
 
-    def conv_row(y, carry):
-        x = ext[pl.ds(y, 3)].reshape(3 * chans, wide)
-        p = jnp.dot(cw_ref[...], x, preferred_element_type=F32)
-        total = (
-            s_ref[y].astype(F32)
-            + p[chans : 2 * chans, :cols]
-            + pltpu.roll(p[:chans], 1, 1)[:, :cols]
-            + pltpu.roll(p[2 * chans :], wide - 1, 1)[:, :cols]
-        )
-        dyn = total.astype(BF)
-        dyn_ref[y] = dyn
-        both = jnp.concatenate([dyn.astype(F32), f_ref[y].astype(F32)], axis=0)
-        feats[pl.ds(pl.multiple_of(y * cols, LANES), cols), :] = both.T
-        return carry
-
-    lax.fori_loop(0, rows, conv_row, 0, unroll=8)
-
     def fetch(g, buf, start, stop):
         base = jnp.minimum(g, groups - 1) * GROUP
-        for r in range(start, stop):
-            buf[pl.ds(r, 1), :] = feats[pl.ds(src[base + r], 1), :]
-
+        for r in range(start, stop, 8):
+            rows8 = feats[pl.ds(src[0, base + r], 8, stride=0), :]
+            for k in range(1, 8):
+                rows8 = jnp.where(sub == k, feats[pl.ds(src[0, base + r + k], 8, stride=0), :], rows8)
+            buf[r : r + 8, :] = rows8
+
+    sub = lax.broadcasted_iota(jnp.int32, (8, LANES), 0)
     ones = jnp.ones((GROUP, LANES), BF)
+
+    each = GROUP // cap
+
+    def outward(i):
+        rows_part = pl.ds(pl.multiple_of(i * 2 * GROUP, GROUP), 2 * GROUP)
+        owner_part = pl.ds(i * 2 * each, 2 * each)
+        return (
+            pltpu.make_async_copy(tend_buf.at[rows_part], tend_ref.at[rows_part], tend_sems.at[i]),
+            pltpu.make_async_copy(send_buf.at[owner_part], send_ref.at[owner_part], send_sems.at[i]),
+        )
 
     def net(g, buf, following):
         part = GROUP // 4
@@ -127,54 +183,74 @@
         h = half_gelu(jnp.dot(h, w3h[...], preferred_element_type=F32) + b3_ref[...] * 0.5)
         fetch(g + 1, following, 3 * part, GROUP)
         out = jnp.dot(h, w4_ref[...], preferred_element_type=F32) + b4_ref[...]
-        tend_ref[pl.ds(pl.multiple_of(g * GROUP, GROUP), GROUP), :] = out.astype(BF)
         flip = out.T[chans:]
-        for j in range(GROUP // cap):
-            o = g * (GROUP // cap) + j
-            diag = jnp.where(vsrc_ref[pl.ds(o, 1), :] < cells, flip[:, j * cap : (j + 1) * cap], 0.0)
-            send_ref[o] = diag.astype(BF)
+        tend_buf[pl.ds(pl.multiple_of(g * GROUP, GROUP), GROUP), :] = out.astype(BF)
+        for j in range(each):
+            at = pl.multiple_of((g * each + j) * cap, LANES)
+            filled = vsrc_ref[:, pl.ds(at, cap)] < cells
+            diag = jnp.where(filled, flip[:, j * cap : (j + 1) * cap], 0.0)
+            send_buf[g * each + j] = diag.astype(BF)
 
     fetch(0, buf0, 0, GROUP)
 
     def pair(i, carry):
         net(2 * i, buf0, buf1)
         net(2 * i + 1, buf1, buf0)
+        for copy in outward(i):
+            copy.start()
         return carry
 
     lax.fori_loop(0, groups // 2, pair, 0)
-
-
-def place_kernel(src, dyn_ref, tend_ref, new_ref, acc, rows_f32):
-    rows, chans, cols = dyn_ref.shape
+    for i in range(groups // 2):
+        for copy in outward(i):
+            copy.wait()
+    for k in range(chunks):
+        dyn_store(k).wait()
+
+
+def place_kernel(src, dyn_any, tend_any, new_ref, acc, rows_f32, dyn_ref, tend_ref, new_wide, sems):
+    chans, rows, cols = new_ref.shape
     slots = tend_ref.shape[0]
-
+    tend_copy = pltpu.make_async_copy(tend_any, tend_ref, sems.at[0])
+    tend_copy.start()
+    dyn_copy = pltpu.make_async_copy(dyn_any, dyn_ref, sems.at[1])
+    dyn_copy.start()
     acc[...] = jnp.zeros(acc.shape, F32)
+    tend_copy.wait()
 
     def block(n, carry):
         base = n * LANES
         rows_f32[...] = tend_ref[pl.ds(pl.multiple_of(base, LANES), LANES), :].astype(F32)
         for r in range(LANES):
-            acc[pl.ds(src[base + r], 1), :] = rows_f32[pl.ds(r, 1), :]
+            acc[pl.ds(src[0, base + r], 1), :] = rows_f32[pl.ds(r, 1), :]
         return carry
 
     lax.fori_loop(0, slots // LANES, block, 0)
+    dyn_copy.wait()
 
     def row(y, carry):
         part = acc[pl.ds(pl.multiple_of(y * cols, LANES), cols), :].T[:chans]
-        new_ref[y] = (dyn_ref[y].astype(F32) + part).astype(BF)
+        total = dyn_ref[y].astype(F32) + part
+        for t in range(cols // LANES):
+            new_wide[t, pl.ds(y, chans, stride=PITCH), :] = total[:, t * LANES : (t + 1) * LANES]
         return carry
 
     lax.fori_loop(0, rows, row, 0, unroll=4)
+    for c in range(chans):
+        for t in range(cols // LANES):
+            part = new_wide[t, c * PITCH : c * PITCH + rows, :]
+            new_ref[c, :, t * LANES : (t + 1) * LANES] = part.astype(BF)
 
 
 def owned_kernel(got_ref, out_ref, wide):
     owners, chans, cap = got_ref.shape
+    pitch = owners + 1
     for h in range(cap // LANES):
         part = slice(h * LANES, (h + 1) * LANES)
         for s in range(owners):
-            wide[h, pl.ds(s, chans, stride=owners), :] = got_ref[s, :, part].astype(F32)
+            wide[h, pl.ds(s, chans, stride=pitch), :] = got_ref[s, :, part].astype(F32)
         for c in range(chans):
-            out_ref[c, :, part] = wide[h, c * owners : (c + 1) * owners, :].astype(BF)
+            out_ref[c, :, part] = wide[h, c * pitch : c * pitch + owners, :].astype(BF)
 
 
 def shift(block, axis, step, periodic):
@@ -194,9 +270,10 @@
     owners = lax.axis_size("lon")
     cap = slots // owners
     wide = cols + LANES
-    src = source.reshape(slots)
+    src = source.reshape(1, slots)
     vmem = pl.BlockSpec(memory_space=pltpu.VMEM)
     smem = pl.BlockSpec(memory_space=pltpu.SMEM)
+    hbm = pl.BlockSpec(memory_space=pltpu.HBM)
 
     tile = (chans, rows, LANES)
     pay = pl.pallas_call(
@@ -214,7 +291,8 @@
     right = shift(pay, "lon", -1, True)
     s = state.transpose(1, 0, 2)
     f = forcing.transpose(1, 0, 2)
-    cw = conv_weight.reshape(3, 3, chans, chans).transpose(1, 2, 0, 3).reshape(3 * chans, 3 * chans)
+    taps = conv_weight.reshape(3, 3, chans, chans)
+    cw = taps.transpose(1, 2, 0, 3).reshape(3 * chans, 3 * chans)
     whole = pl.BlockSpec((rows, LANES), lambda i: (0, 0))
     up, down = pl.pallas_call(
         rows_kernel,
@@ -232,53 +310,72 @@
     top = shift(down, "lat", 1, False)
     bot = shift(up, "lat", -1, False)
 
+    chunks = rows // CHUNK
+    tile_all = (rows, chans, cols)
     dyn, tend, send = pl.pallas_call(
         columns_kernel,
         out_shape=(
-            jax.ShapeDtypeStruct((rows, chans, cols), BF),
+            jax.ShapeDtypeStruct(tile_all, BF),
             jax.ShapeDtypeStruct((slots, 2 * chans), BF),
             jax.ShapeDtypeStruct((owners, chans, cap), BF),
         ),
-        in_specs=[smem] + [vmem] * 16,
-        out_specs=(vmem, vmem, vmem),
+        in_specs=[smem, hbm] + [vmem] * 4 + [hbm, vmem] + [hbm, vmem] * 4 + [vmem],
+        out_specs=(hbm,) * 3,
         scratch_shapes=[
             pltpu.VMEM((rows + 2, chans, wide), BF),
             pltpu.VMEM((cells + 8, 2 * chans), F32),
+            pltpu.VMEM(tile_all, BF),
+            pltpu.VMEM(tile_all, BF),
             pltpu.VMEM((GROUP, 2 * chans), F32),
             pltpu.VMEM((GROUP, 2 * chans), F32),
             pltpu.VMEM((2 * LANES, hid), BF),
             pltpu.VMEM(w_second.shape, BF),
             pltpu.VMEM(w_third.shape, BF),
+            pltpu.VMEM(w_first.shape, BF),
+            pltpu.VMEM(w_second.shape, BF),
+            pltpu.VMEM(w_third.shape, BF),
+            pltpu.VMEM(w_final.shape, BF),
+            pltpu.VMEM((slots, 2 * chans), BF),
+            pltpu.VMEM((owners, chans, cap), BF),
+            pltpu.SemaphoreType.DMA((chunks,)),
+            pltpu.SemaphoreType.DMA((chunks,)),
+            pltpu.SemaphoreType.DMA((chunks,)),
+            pltpu.SemaphoreType.DMA((4,)),
+            pltpu.SemaphoreType.DMA((slots // GROUP // 2,)),
+            pltpu.SemaphoreType.DMA((slots // GROUP // 2,)),
         ],
-        compiler_params=pltpu.CompilerParams(vmem_limit_bytes=40 << 20),
+        compiler_params=pltpu.CompilerParams(vmem_limit_bytes=60 << 20),
         cost_estimate=pl.CostEstimate(flops=10_000_000_000, bytes_accessed=8_000_000, transcendentals=12_000_000),
         name="columns",
     )(
         src, s, left, right, top, bot, f, cw, w_first, b_first.reshape(1, hid), w_second,
         b_second.reshape(1, hid), w_third, b_third.reshape(1, hid), w_final,
-        b_final.reshape(1, 2 * chans), src.reshape(owners, cap),
+        b_final.reshape(1, 2 * chans), src,
     )
     got = lax.all_to_all(send, "lon", split_axis=0, concat_axis=0, tiled=True)
-    new = pl.pallas_call(
+    new_state = pl.pallas_call(
         place_kernel,
-        out_shape=jax.ShapeDtypeStruct((rows, chans, cols), BF),
-        in_specs=[smem, vmem, vmem],
+        out_shape=jax.ShapeDtypeStruct((chans, rows, cols), BF),
+        in_specs=[smem, hbm, hbm],
         out_specs=vmem,
         scratch_shapes=[
             pltpu.VMEM((cells + 8, 2 * chans), F32),
             pltpu.VMEM((LANES, 2 * chans), F32),
+            pltpu.VMEM(tile_all, BF),
+            pltpu.VMEM((slots, 2 * chans), BF),
+            pltpu.VMEM((cols // LANES, chans * PITCH, LANES), F32),
+            pltpu.SemaphoreType.DMA((2,)),
         ],
-        compiler_params=pltpu.CompilerParams(vmem_limit_bytes=32 << 20),
+        compiler_params=pltpu.CompilerParams(vmem_limit_bytes=60 << 20),
         cost_estimate=pl.CostEstimate(flops=5_000_000_000, bytes_accessed=8_000_000, transcendentals=0),
         name="place",
     )(src, dyn, tend)
-    new_state = new.transpose(1, 0, 2)
     owned = pl.pallas_call(
         owned_kernel,
         out_shape=jax.ShapeDtypeStruct((chans, owners, cap), BF),
         in_specs=[vmem],
         out_specs=vmem,
-        scratch_shapes=[pltpu.VMEM((cap // LANES, chans * owners, LANES), F32)],
+        scratch_shapes=[pltpu.VMEM((cap // LANES, chans * (owners + 1), LANES), F32)],
         compiler_params=pltpu.CompilerParams(vmem_limit_bytes=16 << 20),
         name="owned",
     )(got)

time: 81.9 us -> 79.8 us (0.974)
  local copies, waits for them, and re-layouts: 8.53 us -> 5.55 us
  Pallas kernels: 45.3 us -> 46.3 us
    unnamed x42 -> x16, local copies, waits for them, and re-layouts: 8.23 us -> 4.62 us
    pallas_call x2, Pallas kernels: 38 us -> 40.9 us  [the longest x1 27.8 us: body(): pl.pallas_call(columns_kernel, out_shape=(jax.ShapeDtypeStruct(tile_all,...]
    pallas_call x1, Pallas kernels: 3.16 us -> 1.25 us  [body(): pl.pallas_call(owned_kernel, out_shape=jax.ShapeDtypeStruct((chans, owner...]
    all_to_all x1, waiting for transfers between devices: 3.14 us -> 3.96 us  [body(): got = lax.all_to_all(send, 'lon', split_axis=0, concat_axis=0, tiled=True)]
  transfers between devices with their start and end apart: 5 -> 5, of which waited for: 3 -> 3; matrix products, arithmetic and copies ran while one was open for 7% -> 6% of each run, Pallas kernels for 13% -> 17%
where the time goes in v3:
time: 79.8 us; the launch traced here: 78.5 us
  Pallas kernels  46.3 us (58%)
  starting transfers between devices  18.2 us (23%)
  waiting for transfers between devices  7.77 us (10%)
  local copies, waits for them, and re-layouts  5.55 us (7%)
    pallas_call x1, Pallas kernels, body(): pl.pallas_call(columns_kernel, out_shape=(jax.ShapeDtypeStruct(tile_all,...  27.8 us
    pallas_call x1, Pallas kernels, body(): pl.pallas_call(place_kernel, out_shape=jax.ShapeDtypeStruct((chans, rows,...  13 us
    all_to_all x1, starting transfers between devices, body(): got = lax.all_to_all(send, 'lon', split_axis=0, concat_axis=0, tiled=True)  10.7 us
    ppermute x4, starting transfers between devices, shift(): return lax.ppermute(block, axis, pairs)  7.47 us
    unnamed x16, local copies, waits for them, and re-layouts  4.62 us
    all_to_all x1, waiting for transfers between devices, body(): got = lax.all_to_all(send, 'lon', split_axis=0, concat_axis=0, tiled=True)  3.96 us
    ppermute x4, waiting for transfers between devices, shift(): return lax.ppermute(block, axis, pairs)  3.81 us
    pallas_call x1, Pallas kernels, body(): pl.pallas_call(edges_kernel, grid=(1,), out_shape=jax.ShapeDtypeStruct((r...  2.39 us
  transfers between devices with their start and end apart: 5, of which 3 were waited for; matrix products, arithmetic and copies ran while one was open for 6% of the time, Pallas kernels for 17%

profile of v3, /device:TPU:9, one launch (start us, length us, event | category | flops | bytes accessed | tf_op | source)
XLA Modules:
  0.0 78.5 jit_solution(16146886343307319001)
XLA Ops:
  0.6 0.0 copy-start
  0.6 2.4 %edges.1 = bf16[32,128]{1,0:T(8,128)(2,1)} custom-call(bf16[64,32,384]{2,1,0:T(8,128)(2,1)} %high_ref.1, bf16[64,32,384]{2,1,0:T(8,128)(2,1)} %high_ref.1), custom_call_target="tpu_custom_call" | custom-call | tf_op jit(solution)/shard_map/edges/pallas_call | solution.py:279
  3.0 0.7 collective-permute-start.1
  3.7 1.5 %collective-permute-start = (bf16[32,128]{1,0:T(8,128)(2,1)}, bf16[32,128]{1,0:T(8,128)(2,1)S(1)}, u32[]{:S(2)}, u32[]{:S(2)}) collective-permute-start(bf16[32,128]{1,0:T(8,128)(2,1)} %edges.1), channel_id=1, source_target_pairs={{0,1},{1,2},{2,3},{3,4},{4,5},{5,6},{6,7},{7,8},{8,9},{9,10},{10,1... | collective-permute-start | bytes 24584 | tf_op jit(solution)/shard_map/ppermute | solution.py:259
  5.2 0.0 copy-done
  5.2 1.7 %copy.26 = bf16[64,32,384]{2,0,1:T(8,128)(2,1)} copy(bf16[64,32,384]{2,1,0:T(8,128)(2,1)S(1)} %copy-done) | data formatting | bytes 3145728 | tf_op args[0]
  6.9 0.0 collective-permute-done.1.right_ref
  6.9 0.0 copy-start.3
  6.9 3.3 %collective-permute-done.left_ref = bf16[32,128]{1,0:T(8,128)(2,1)S(1)} collective-permute-done((bf16[32,128]{1,0:T(8,128)(2,1)}, bf16[32,128]{1,0:T(8,128)(2,1)S(1)}, u32[]{:S(2)}, u32[]{:S(2)}) %collective-permute-start) | collective-permute-done | bytes 8224 | tf_op jit(solution)/shard_map/ppermute | solution.py:259
  10.3 0.0 copy-start.4
  10.3 0.0 copy-done.3
  10.3 0.6 copy-done.4
  10.9 0.0 copy-start.2
  10.9 0.0 copy-start.1
  10.9 1.8 %rows.1 = (bf16[64,512]{1,0:T(8,128)(2,1)}, bf16[64,512]{1,0:T(8,128)(2,1)}) custom-call(bf16[32,128]{1,0:T(8,128)(2,1)} %copy-done.4, bf16[32,128]{1,0:T(8,128)(2,1)} %copy-done.3, bf16[32,64,384]{2,1,0:T(8,128)(2,1)} %bitcast.18, bf16[32,64,384]{2,1,0:T(8,128)(2,1)} %bitcast.19), custom_call_target="tpu_custom_call" | custom-call | tf_op jit(solution)/shard_map/rows/pallas_call | solution.py:297
  12.7 3.2 %collective-permute-start.2 = (bf16[64,512]{1,0:T(8,128)(2,1)}, bf16[64,512]{1,0:T(8,128)(2,1)S(1)}, u32[]{:S(2)}, u32[]{:S(2)}) collective-permute-start(bf16[64,512]{1,0:T(8,128)(2,1)} %get-tuple-element.7), channel_id=1, source_target_pairs={{0,32},{32,64},{64,96},{1,33},{33,65},{65,97},{2,34},{34,66},{66,9... | collective-permute-start | bytes 196616 | tf_op jit(solution)/shard_map/ppermute | solution.py:259
  15.9 2.1 %collective-permute-start.3 = (bf16[64,512]{1,0:T(8,128)(2,1)}, bf16[64,512]{1,0:T(8,128)(2,1)S(1)}, u32[]{:S(2)}, u32[]{:S(2)}) collective-permute-start(bf16[64,512]{1,0:T(8,128)(2,1)} %get-tuple-element.8), channel_id=1, source_target_pairs={{32,0},{64,32},{96,64},{33,1},{65,33},{97,65},{34,2},{66,34},{98,6... | collective-permute-start | bytes 196616 | tf_op jit(solution)/shard_map/ppermute | solution.py:259
  17.9 0.0 copy-done.2
  18.0 0.1 copy.27
  18.1 0.8 %reshape.30.cw_ref = bf16[192,192]{1,0:T(8,128)(2,1)} reshape(bf16[3,64,3,64]{3,2,1,0:T(4,128)(2,1)S(1)} %bitcast.23) | data formatting | bytes 147456 | tf_op jit(solution)/shard_map/reshape | solution.py:295
  18.9 0.0 copy-done.1
  18.9 1.7 %copy.25 = bf16[64,32,384]{2,0,1:T(8,128)(2,1)} copy(bf16[64,32,384]{2,1,0:T(8,128)(2,1)S(1)} %copy-done.1) | data formatting | bytes 3145728 | tf_op args[1]
  20.6 0.0 collective-permute-done.2.top_ref
  20.6 0.0 copy-start.5
  20.6 0.5 collective-permute-done.3.bot_ref
  21.1 0.0 copy-start.6
  21.1 0.2 copy-done.5
  21.3 0.5 copy-done.6
  21.7 27.8 %columns.1 = (bf16[32,64,384]{2,1,0:T(8,128)(2,1)}, bf16[8192,128]{1,0:T(8,128)(2,1)}, bf16[32,64,256]{2,1,0:T(8,128)(2,1)}) custom-call(s32[1,8192]{1,0:T(1,128)} %bitcast.25, bf16[32,64,384]{2,1,0:T(8,128)(2,1)} %bitcast.20, bf16[32,128]{1,0:T(8,128)(2,1)} %copy-done.4, bf16[32,128]{1,0:T(8,128)(2,1)} %copy-done.3, bf16[64,512]{1,0:T(8,128)(2,1)} %copy-done.5, ...), custom_call_target="tpu_custom_call" | custom-call | flops 10000000000 | bytes 8000000 | tf_op jit(solution)/shard_map/columns/pallas_call | solution.py:315
  49.5 10.7 %all-to-all-start = ((bf16[32,64,256]{2,1,0:T(8,128)(2,1)}), bf16[32,64,256]{2,1,0:T(8,128)(2,1)S(1)}, u32[]{:S(2)}, u32[]{:S(2)}) async-start(bf16[32,64,256]{2,1,0:T(8,128)(2,1)} %get-tuple-element.11), calls=%async_computation | async-start | bytes 2097152 | tf_op jit(solution)/shard_map/all_to_all | solution.py:355
  60.3 13.0 %place.1 = bf16[64,32,384]{2,1,0:T(8,128)(2,1)} custom-call(s32[1,8192]{1,0:T(1,128)} %bitcast.27, bf16[32,64,384]{2,1,0:T(8,128)(2,1)} %get-tuple-element.9.dyn_any, bf16[8192,128]{1,0:T(8,128)(2,1)} %get-tuple-element.10.tend_any), custom_call_target="tpu_custom_call" | custom-call | flops 5000000000 | bytes 8000000 | tf_op jit(solution)/shard_map/place/pallas_call | solution.py:356
  73.3 4.0 %all-to-all-done.got_ref = bf16[32,64,256]{2,1,0:T(8,128)(2,1)S(1)} async-done(((bf16[32,64,256]{2,1,0:T(8,128)(2,1)}), bf16[32,64,256]{2,1,0:T(8,128)(2,1)S(1)}, u32[]{:S(2)}, u32[]{:S(2)}) %all-to-all-start) | async-done | bytes 1048608 | tf_op jit(solution)/shard_map/all_to_all | solution.py:355
  77.3 1.2 %owned.1 = bf16[64,32,256]{2,1,0:T(8,128)(2,1)} custom-call(bf16[32,64,256]{2,1,0:T(8,128)(2,1)S(1)} %all-to-all-done.got_ref), custom_call_target="tpu_custom_call" | custom-call | tf_op jit(solution)/shard_map/owned/pallas_call | solution.py:373
Async XLA Ops:
  0.6 4.6 %copy-start = (bf16[64,32,384]{2,1,0:T(8,128)(2,1)S(1)}, bf16[64,32,384]{2,1,0:T(8,128)(2,1)}, u32[]{:S(2)}) copy-start(bf16[64,32,384]{2,1,0:T(8,128)(2,1)} %high_ref.1) | copy-start | bytes 4718596
  3.0 3.9 %collective-permute-start.1 = (bf16[32,128]{1,0:T(8,128)(2,1)}, bf16[32,128]{1,0:T(8,128)(2,1)S(1)}, u32[]{:S(2)}, u32[]{:S(2)}) collective-permute-start(bf16[32,128]{1,0:T(8,128)(2,1)} %edges.1), channel_id=1, source_target_pairs={{0,31},{1,0},{2,1},{3,2},{4,3},{5,4},{6,5},{7,6},{8,7},{9,8},{10,9... | collective-permute-start | bytes 24584 | tf_op jit(solution)/shard_map/ppermute | solution.py:259
  3.7 6.5 %collective-permute-start = (bf16[32,128]{1,0:T(8,128)(2,1)}, bf16[32,128]{1,0:T(8,128)(2,1)S(1)}, u32[]{:S(2)}, u32[]{:S(2)}) collective-permute-start(bf16[32,128]{1,0:T(8,128)(2,1)} %edges.1), channel_id=1, source_target_pairs={{0,1},{1,2},{2,3},{3,4},{4,5},{5,6},{6,7},{7,8},{8,9},{9,10},{10,1... | collective-permute-start | bytes 24584 | tf_op jit(solution)/shard_map/ppermute | solution.py:259
  6.9 3.3 %copy-start.3 = (bf16[32,128]{1,0:T(8,128)(2,1)}, bf16[32,128]{1,0:T(8,128)(2,1)S(1)}, u32[]{:S(2)}) copy-start(bf16[32,128]{1,0:T(8,128)(2,1)S(1)} %collective-permute-done.1.right_ref) | copy-start | bytes 24580
  10.3 0.6 copy-start.4
  10.9 7.1 %copy-start.2 = (bf16[9,64,64]{2,1,0:T(8,128)(2,1)S(1)}, bf16[9,64,64]{2,1,0:T(8,128)(2,1)}, u32[]{:S(2)}) copy-start(bf16[9,64,64]{2,1,0:T(8,128)(2,1)} %param.17) | copy-start | bytes 221188
  10.9 8.0 %copy-start.1 = (bf16[64,32,384]{2,1,0:T(8,128)(2,1)S(1)}, bf16[64,32,384]{2,1,0:T(8,128)(2,1)}, u32[]{:S(2)}) copy-start(bf16[64,32,384]{2,1,0:T(8,128)(2,1)} %param.16) | copy-start | bytes 4718596
  12.7 7.9 %collective-permute-start.2 = (bf16[64,512]{1,0:T(8,128)(2,1)}, bf16[64,512]{1,0:T(8,128)(2,1)S(1)}, u32[]{:S(2)}, u32[]{:S(2)}) collective-permute-start(bf16[64,512]{1,0:T(8,128)(2,1)} %get-tuple-element.7), channel_id=1, source_target_pairs={{0,32},{32,64},{64,96},{1,33},{33,65},{65,97},{2,34},{34,66},{66,9... | collective-permute-start | bytes 196616 | tf_op jit(solution)/shard_map/ppermute | solution.py:259
  15.9 5.2 %collective-permute-start.3 = (bf16[64,512]{1,0:T(8,128)(2,1)}, bf16[64,512]{1,0:T(8,128)(2,1)S(1)}, u32[]{:S(2)}, u32[]{:S(2)}) collective-permute-start(bf16[64,512]{1,0:T(8,128)(2,1)} %get-tuple-element.8), channel_id=1, source_target_pairs={{32,0},{64,32},{96,64},{33,1},{65,33},{97,65},{34,2},{66,34},{98,6... | collective-permute-start | bytes 196616 | tf_op jit(solution)/shard_map/ppermute | solution.py:259
  20.6 0.6 copy-start.5
  21.1 0.6 copy-start.6
  49.5 27.7 %all-to-all-start = ((bf16[32,64,256]{2,1,0:T(8,128)(2,1)}), bf16[32,64,256]{2,1,0:T(8,128)(2,1)S(1)}, u32[]{:S(2)}, u32[]{:S(2)}) async-start(bf16[32,64,256]{2,1,0:T(8,128)(2,1)} %get-tuple-element.11), calls=%async_computation | async-start | bytes 2097152 | tf_op jit(solution)/shard_map/all_to_all | solution.py:355

commit v4 on v3

--- a/solution.py
+++ b/solution.py
@@ -61,11 +61,12 @@
 
 
 def columns_kernel(
-    src, s_any, left_ref, right_ref, top_ref, bot_ref, f_any, cw_ref,
-    w1_any, b1_ref, w2_any, b2_ref, w3_any, b3_ref, w4_any, b4_ref, vsrc_ref,
+    src_any, s_any, left_any, right_any, top_any, bot_any, f_any, cw_any,
+    w1_any, b1_any, w2_any, b2_any, w3_any, b3_any, w4_any, b4_any,
     dyn_any, tend_ref, send_ref,
-    ext, feats, f_ref, dyn_ref, buf0, buf1, w1h, w2h, w3h, w1_ref, w2_ref, w3_ref, w4_ref,
-    tend_buf, send_buf, s_sems, f_sems, dyn_sems, w_sems, tend_sems, send_sems,
+    src, vsrc_ref, left_ref, right_ref, cw_ref, ext, feats, f_ref, dyn_ref, buf0, buf1, w1h, w2h, w3h,
+    w1_ref, w2_ref, w3_ref, w4_ref, b1_ref, b2_ref, b3_ref, b4_ref,
+    tend_buf, send_buf, s_sems, f_sems, dyn_sems, first_sems, w_sems, tend_sems, send_sems,
 ):
     rows, chans, cols = f_ref.shape
     cells = rows * cols
@@ -88,19 +89,44 @@
         part = pl.ds(k * CHUNK, CHUNK)
         return pltpu.make_async_copy(dyn_ref.at[part], dyn_any.at[part], dyn_sems.at[k])
 
+    firsts = [
+        pltpu.make_async_copy(source, target, first_sems.at[k])
+        for k, (source, target) in enumerate(
+            (
+                (left_any, left_ref),
+                (right_any, right_ref),
+                (cw_any, cw_ref),
+                (top_any, ext.at[0]),
+                (bot_any, ext.at[rows + 1]),
+            )
+        )
+    ]
+    loads = [
+        pltpu.make_async_copy(source, target, w_sems.at[k])
+        for k, (source, target) in enumerate(
+            (
+                (src_any, src),
+                (src_any, vsrc_ref),
+                (w1_any, w1_ref),
+                (b1_any, b1_ref),
+                (w2_any, w2_ref),
+                (b2_any, b2_ref),
+                (w3_any, w3_ref),
+                (b3_any, b3_ref),
+                (w4_any, w4_ref),
+                (b4_any, b4_ref),
+            )
+        )
+    ]
+    for load in firsts:
+        load.start()
     for k in range(chunks):
         s_load(k).start()
         f_load(k).start()
-    loads = [
-        pltpu.make_async_copy(source, target, w_sems.at[k])
-        for k, (source, target) in enumerate(
-            ((w1_any, w1_ref), (w2_any, w2_ref), (w3_any, w3_ref), (w4_any, w4_ref))
-        )
-    ]
     for load in loads:
         load.start()
-    ext[0] = top_ref[...]
-    ext[rows + 1] = bot_ref[...]
+    for load in firsts:
+        load.wait()
     left, right = halo_columns(left_ref, right_ref, chans)
     for y in range(rows):
         ext[y + 1, :, cols:] = halo_tile(left, right, y, chans)
@@ -164,12 +190,16 @@
 
     each = GROUP // cap
 
-    def outward(i):
-        rows_part = pl.ds(pl.multiple_of(i * 2 * GROUP, GROUP), 2 * GROUP)
-        owner_part = pl.ds(i * 2 * each, 2 * each)
+    pairs = groups // 2
+    stages = ((0, pairs - 1), (pairs - 1, pairs))
+
+    def outward(n):
+        start, stop = stages[n]
+        rows_part = pl.ds(start * 2 * GROUP, (stop - start) * 2 * GROUP)
+        owner_part = pl.ds(start * 2 * each, (stop - start) * 2 * each)
         return (
-            pltpu.make_async_copy(tend_buf.at[rows_part], tend_ref.at[rows_part], tend_sems.at[i]),
-            pltpu.make_async_copy(send_buf.at[owner_part], send_ref.at[owner_part], send_sems.at[i]),
+            pltpu.make_async_copy(tend_buf.at[rows_part], tend_ref.at[rows_part], tend_sems.at[n]),
+            pltpu.make_async_copy(send_buf.at[owner_part], send_ref.at[owner_part], send_sems.at[n]),
         )
 
     def net(g, buf, following):
@@ -196,13 +226,14 @@
     def pair(i, carry):
         net(2 * i, buf0, buf1)
         net(2 * i + 1, buf1, buf0)
-        for copy in outward(i):
+        return carry
+
+    for n, (start, stop) in enumerate(stages):
+        lax.fori_loop(start, stop, pair, 0)
+        for copy in outward(n):
             copy.start()
-        return carry
-
-    lax.fori_loop(0, groups // 2, pair, 0)
-    for i in range(groups // 2):
-        for copy in outward(i):
+    for n in range(len(stages)):
+        for copy in outward(n):
             copy.wait()
     for k in range(chunks):
         dyn_store(k).wait()
@@ -285,6 +316,7 @@
             pl.BlockSpec(tile, lambda i: (0, 0, cols // LANES - 1)),
         ],
         out_specs=pl.BlockSpec((rows, LANES), lambda i: (0, 0)),
+        compiler_params=pltpu.CompilerParams(vmem_limit_bytes=8 << 20),
         name="edges",
     )(state, state)
     left = shift(pay, "lon", 1, True)
@@ -305,6 +337,7 @@
             pl.BlockSpec((1, chans, cols), lambda i: (rows - 1, 0, 0)),
         ],
         out_specs=(pl.BlockSpec((chans, wide), lambda i: (0, 0)),) * 2,
+        compiler_params=pltpu.CompilerParams(vmem_limit_bytes=4 << 20),
         name="rows",
     )(left, right, s, s)
     top = shift(down, "lat", 1, False)
@@ -319,9 +352,14 @@
             jax.ShapeDtypeStruct((slots, 2 * chans), BF),
             jax.ShapeDtypeStruct((owners, chans, cap), BF),
         ),
-        in_specs=[smem, hbm] + [vmem] * 4 + [hbm, vmem] + [hbm, vmem] * 4 + [vmem],
+        in_specs=[hbm] * 16,
         out_specs=(hbm,) * 3,
         scratch_shapes=[
+            pltpu.SMEM((1, slots), jnp.int32),
+            pltpu.VMEM((1, slots), jnp.int32),
+            pltpu.VMEM((rows, LANES), BF),
+            pltpu.VMEM((rows, LANES), BF),
+            pltpu.VMEM(cw.shape, BF),
             pltpu.VMEM((rows + 2, chans, wide), BF),
             pltpu.VMEM((cells + 8, 2 * chans), F32),
             pltpu.VMEM(tile_all, BF),
@@ -335,14 +373,19 @@
             pltpu.VMEM(w_second.shape, BF),
             pltpu.VMEM(w_third.shape, BF),
             pltpu.VMEM(w_final.shape, BF),
+            pltpu.VMEM((1, hid), F32),
+            pltpu.VMEM((1, hid), F32),
+            pltpu.VMEM((1, hid), F32),
+            pltpu.VMEM((1, 2 * chans), F32),
             pltpu.VMEM((slots, 2 * chans), BF),
             pltpu.VMEM((owners, chans, cap), BF),
             pltpu.SemaphoreType.DMA((chunks,)),
             pltpu.SemaphoreType.DMA((chunks,)),
             pltpu.SemaphoreType.DMA((chunks,)),
-            pltpu.SemaphoreType.DMA((4,)),
-            pltpu.SemaphoreType.DMA((slots // GROUP // 2,)),
-            pltpu.SemaphoreType.DMA((slots // GROUP // 2,)),
+            pltpu.SemaphoreType.DMA((5,)),
+            pltpu.SemaphoreType.DMA((10,)),
+            pltpu.SemaphoreType.DMA((2,)),
+            pltpu.SemaphoreType.DMA((2,)),
         ],
         compiler_params=pltpu.CompilerParams(vmem_limit_bytes=60 << 20),
         cost_estimate=pl.CostEstimate(flops=10_000_000_000, bytes_accessed=8_000_000, transcendentals=12_000_000),
@@ -350,7 +393,7 @@
     )(
         src, s, left, right, top, bot, f, cw, w_first, b_first.reshape(1, hid), w_second,
         b_second.reshape(1, hid), w_third, b_third.reshape(1, hid), w_final,
-        b_final.reshape(1, 2 * chans), src,
+        b_final.reshape(1, 2 * chans),
     )
     got = lax.all_to_all(send, "lon", split_axis=0, concat_axis=0, tiled=True)
     new_state = pl.pallas_call(

time: 79.8 us -> 76 us (0.952)
  Pallas kernels: 46.3 us -> 41.6 us
    pallas_call x1, Pallas kernels: 2.39 us -> 0.5 us  [body(): pl.pallas_call(edges_kernel, grid=(1,), out_shape=jax.ShapeDtypeStruct((r...]
    pallas_call x1, Pallas kernels: 1.8 us -> 0.18 us  [body(): pl.pallas_call(rows_kernel, grid=(1,), out_shape=(jax.ShapeDtypeStruct((c...]
    pallas_call x1, Pallas kernels: 27.8 us -> 26.6 us  [body(): pl.pallas_call(columns_kernel, out_shape=(jax.ShapeDtypeStruct(tile_all,...]
    unnamed x16 -> x20, local copies, waits for them, and re-layouts: 4.62 us -> 4.69 us
  transfers between devices with their start and end apart: 5 -> 5, of which waited for: 3 -> 4; matrix products, arithmetic and copies ran while one was open for 6% -> 4% of each run, Pallas kernels for 17% -> 17%
where the time goes in v4:
time: 76 us; the launch traced here: 74.7 us
  Pallas kernels  41.6 us (55%)
  starting transfers between devices  18.4 us (24%)
  waiting for transfers between devices  8.36 us (11%)
  local copies, waits for them, and re-layouts  5.65 us (7%)
    pallas_call x1, Pallas kernels, body(): pl.pallas_call(columns_kernel, out_shape=(jax.ShapeDtypeStruct(tile_all,...  26.6 us
    pallas_call x1, Pallas kernels, body(): pl.pallas_call(place_kernel, out_shape=jax.ShapeDtypeStruct((chans, rows,...  13 us
    all_to_all x1, starting transfers between devices, body(): got = lax.all_to_all(send, 'lon', split_axis=0, concat_axis=0, tiled=True)  10.8 us
    ppermute x4, starting transfers between devices, shift(): return lax.ppermute(block, axis, pairs)  7.62 us
    unnamed x20, local copies, waits for them, and re-layouts  4.69 us
    ppermute x4, waiting for transfers between devices, shift(): return lax.ppermute(block, axis, pairs)  4.4 us
    all_to_all x1, waiting for transfers between devices, body(): got = lax.all_to_all(send, 'lon', split_axis=0, concat_axis=0, tiled=True)  3.96 us
  transfers between devices with their start and end apart: 5, of which 4 were waited for; matrix products, arithmetic and copies ran while one was open for 4% of the time, Pallas kernels for 17%

profile of v4, /device:TPU:9, one launch (start us, length us, event | category | flops | bytes accessed | tf_op | source)
XLA Modules:
  0.0 74.7 jit_solution(4735321386610289474)
XLA Ops:
  0.6 0.0 copy-start
  0.6 1.4 %copy-done = bf16[64,32,384]{2,1,0:T(8,128)(2,1)S(1)} copy-done((bf16[64,32,384]{2,1,0:T(8,128)(2,1)S(1)}, bf16[64,32,384]{2,1,0:T(8,128)(2,1)}, u32[]{:S(2)}) %copy-start) | copy-done | bytes 1572888
  2.0 0.0 copy-start.1
  2.0 0.5 edges.1
  2.5 0.7 collective-permute-start.1
  3.3 1.6 %collective-permute-start = (bf16[32,128]{1,0:T(8,128)(2,1)S(1)}, bf16[32,128]{1,0:T(8,128)(2,1)S(1)}, u32[]{:S(2)}, u32[]{:S(2)}) collective-permute-start(bf16[32,128]{1,0:T(8,128)(2,1)S(1)} %edges.1), channel_id=1, source_target_pairs={{0,1},{1,2},{2,3},{3,4},{4,5},{5,6},{6,7},{7,8},{8,9},{9,10},{10,1... | collective-permute-start | bytes 24584 | tf_op jit(solution)/shard_map/ppermute | solution.py:290
  4.9 0.0 copy-done.1
  4.9 0.6 copy.26
  5.5 0.0 copy-start.2
  5.5 0.7 collective-permute-done.1.right_ref.right_any
  6.1 0.0 copy-start.3
  6.2 3.5 %collective-permute-done.left_ref.left_any = bf16[32,128]{1,0:T(8,128)(2,1)S(1)} collective-permute-done((bf16[32,128]{1,0:T(8,128)(2,1)S(1)}, bf16[32,128]{1,0:T(8,128)(2,1)S(1)}, u32[]{:S(2)}, u32[]{:S(2)}) %collective-permute-start) | collective-permute-done | bytes 8224 | tf_op jit(solution)/shard_map/ppermute | solution.py:290
  9.6 0.0 copy-start.4
  9.6 0.0 copy-start.6
  9.6 0.0 copy-start.5
  9.6 0.2 rows.1
  9.8 0.0 copy-done.2
  9.8 0.0 copy-done.3
  9.8 0.4 copy-done.4
  10.2 3.2 %collective-permute-start.2 = (bf16[64,512]{1,0:T(8,128)(2,1)S(1)}, bf16[64,512]{1,0:T(8,128)(2,1)S(1)}, u32[]{:S(2)}, u32[]{:S(2)}) collective-permute-start(bf16[64,512]{1,0:T(8,128)(2,1)S(1)} %get-tuple-element.7), channel_id=1, source_target_pairs={{0,32},{32,64},{64,96},{1,33},{33,65},{65,97},{2,34},{34,66},{66,9... | collective-permute-start | bytes 196616 | tf_op jit(solution)/shard_map/ppermute | solution.py:290
  13.4 2.1 %collective-permute-start.3 = (bf16[64,512]{1,0:T(8,128)(2,1)S(1)}, bf16[64,512]{1,0:T(8,128)(2,1)S(1)}, u32[]{:S(2)}, u32[]{:S(2)}) collective-permute-start(bf16[64,512]{1,0:T(8,128)(2,1)S(1)} %get-tuple-element.8), channel_id=1, source_target_pairs={{32,0},{64,32},{96,64},{33,1},{65,33},{97,65},{34,2},{66,34},{98,6... | collective-permute-start | bytes 196616 | tf_op jit(solution)/shard_map/ppermute | solution.py:290
  15.5 0.0 copy-done.6
  15.5 0.1 copy.27
  15.7 0.8 %reshape.30.cw_any = bf16[192,192]{1,0:T(8,128)(2,1)} reshape(bf16[3,64,3,64]{3,2,1,0:T(4,128)(2,1)S(1)} %bitcast.23) | data formatting | bytes 147456 | tf_op jit(solution)/shard_map/reshape | solution.py:327
  16.5 0.0 copy-done.5
  16.5 1.7 %copy.25 = bf16[64,32,384]{2,0,1:T(8,128)(2,1)} copy(bf16[64,32,384]{2,1,0:T(8,128)(2,1)S(1)} %copy-done.5) | data formatting | bytes 3145728 | tf_op args[1]
  18.2 0.0 collective-permute-done.2.top_any
  18.2 0.0 copy-start.7
  18.2 0.2 collective-permute-done.3.bot_any
  18.4 0.0 copy-start.8
  18.4 0.4 copy-done.7
  18.8 0.2 copy-done.8
  19.1 26.6 %columns.1 = (bf16[32,64,384]{2,1,0:T(8,128)(2,1)}, bf16[8192,128]{1,0:T(8,128)(2,1)}, bf16[32,64,256]{2,1,0:T(8,128)(2,1)}) custom-call(s32[1,8192]{1,0:T(1,128)} %bitcast.25, bf16[32,64,384]{2,1,0:T(8,128)(2,1)} %bitcast.20, bf16[32,128]{1,0:T(8,128)(2,1)} %copy-done.4, bf16[32,128]{1,0:T(8,128)(2,1)} %copy-done.3, bf16[64,512]{1,0:T(8,128)(2,1)} %copy-done.7, ...), custom_call_target="tpu_custom_call" | custom-call | flops 10000000000 | bytes 8000000 | tf_op jit(solution)/shard_map/columns/pallas_call | solution.py:348
  45.7 10.8 %all-to-all-start = ((bf16[32,64,256]{2,1,0:T(8,128)(2,1)}), bf16[32,64,256]{2,1,0:T(8,128)(2,1)S(1)}, u32[]{:S(2)}, u32[]{:S(2)}) async-start(bf16[32,64,256]{2,1,0:T(8,128)(2,1)} %get-tuple-element.11), calls=%async_computation | async-start | bytes 2097152 | tf_op jit(solution)/shard_map/all_to_all | solution.py:398
  56.5 13.0 %place.1 = bf16[64,32,384]{2,1,0:T(8,128)(2,1)} custom-call(s32[1,8192]{1,0:T(1,128)} %bitcast.26, bf16[32,64,384]{2,1,0:T(8,128)(2,1)} %get-tuple-element.9.dyn_any, bf16[8192,128]{1,0:T(8,128)(2,1)} %get-tuple-element.10.tend_any), custom_call_target="tpu_custom_call" | custom-call | flops 5000000000 | bytes 8000000 | tf_op jit(solution)/shard_map/place/pallas_call | solution.py:399
  69.5 4.0 %all-to-all-done.got_ref = bf16[32,64,256]{2,1,0:T(8,128)(2,1)S(1)} async-done(((bf16[32,64,256]{2,1,0:T(8,128)(2,1)}), bf16[32,64,256]{2,1,0:T(8,128)(2,1)S(1)}, u32[]{:S(2)}, u32[]{:S(2)}) %all-to-all-start) | async-done | bytes 1048608 | tf_op jit(solution)/shard_map/all_to_all | solution.py:398
  73.5 1.2 %owned.1 = bf16[64,32,256]{2,1,0:T(8,128)(2,1)} custom-call(bf16[32,64,256]{2,1,0:T(8,128)(2,1)S(1)} %all-to-all-done.got_ref), custom_call_target="tpu_custom_call" | custom-call | tf_op jit(solution)/shard_map/owned/pallas_call | solution.py:416
Async XLA Ops:
  0.6 1.4 %copy-start = (bf16[64,32,384]{2,1,0:T(8,128)(2,1)S(1)}, bf16[64,32,384]{2,1,0:T(8,128)(2,1)}, u32[]{:S(2)}) copy-start(bf16[64,32,384]{2,1,0:T(8,128)(2,1)} %high_ref.1) | copy-start | bytes 4718596
  2.0 2.9 %copy-start.1 = (bf16[64,32,384]{2,1,0:T(8,128)(2,1)S(1)}, bf16[64,32,384]{2,1,0:T(8,128)(2,1)}, u32[]{:S(2)}) copy-start(bf16[64,32,384]{2,1,0:T(8,128)(2,1)} %high_ref.1) | copy-start | bytes 4718596
  2.5 3.6 %collective-permute-start.1 = (bf16[32,128]{1,0:T(8,128)(2,1)S(1)}, bf16[32,128]{1,0:T(8,128)(2,1)S(1)}, u32[]{:S(2)}, u32[]{:S(2)}) collective-permute-start(bf16[32,128]{1,0:T(8,128)(2,1)S(1)} %edges.1), channel_id=1, source_target_pairs={{0,31},{1,0},{2,1},{3,2},{4,3},{5,4},{6,5},{7,6},{8,7},{9,8},{10,9... | collective-permute-start | bytes 24584 | tf_op jit(solution)/shard_map/ppermute | solution.py:290
  3.3 6.3 %collective-permute-start = (bf16[32,128]{1,0:T(8,128)(2,1)S(1)}, bf16[32,128]{1,0:T(8,128)(2,1)S(1)}, u32[]{:S(2)}, u32[]{:S(2)}) collective-permute-start(bf16[32,128]{1,0:T(8,128)(2,1)S(1)} %edges.1), channel_id=1, source_target_pairs={{0,1},{1,2},{2,3},{3,4},{4,5},{5,6},{6,7},{7,8},{8,9},{9,10},{10,1... | collective-permute-start | bytes 24584 | tf_op jit(solution)/shard_map/ppermute | solution.py:290
  5.5 4.4 %copy-start.2 = (bf16[64,32,384]{2,0,1:T(8,128)(2,1)}, bf16[64,32,384]{2,0,1:T(8,128)(2,1)S(1)}, u32[]{:S(2)}) copy-start(bf16[64,32,384]{2,0,1:T(8,128)(2,1)S(1)} %copy.26) | copy-start | bytes 4718596
  6.1 3.7 %copy-start.3 = (bf16[32,128]{1,0:T(8,128)(2,1)}, bf16[32,128]{1,0:T(8,128)(2,1)S(1)}, u32[]{:S(2)}) copy-start(bf16[32,128]{1,0:T(8,128)(2,1)S(1)} %collective-permute-done.1.right_ref.right_any) | copy-start | bytes 24580
  9.6 0.6 copy-start.4
  9.6 5.9 %copy-start.6 = (bf16[9,64,64]{2,1,0:T(8,128)(2,1)S(1)}, bf16[9,64,64]{2,1,0:T(8,128)(2,1)}, u32[]{:S(2)}) copy-start(bf16[9,64,64]{2,1,0:T(8,128)(2,1)} %param.17) | copy-start | bytes 221188
  9.6 6.9 %copy-start.5 = (bf16[64,32,384]{2,1,0:T(8,128)(2,1)S(1)}, bf16[64,32,384]{2,1,0:T(8,128)(2,1)}, u32[]{:S(2)}) copy-start(bf16[64,32,384]{2,1,0:T(8,128)(2,1)} %param.16) | copy-start | bytes 4718596
  10.2 8.0 %collective-permute-start.2 = (bf16[64,512]{1,0:T(8,128)(2,1)S(1)}, bf16[64,512]{1,0:T(8,128)(2,1)S(1)}, u32[]{:S(2)}, u32[]{:S(2)}) collective-permute-start(bf16[64,512]{1,0:T(8,128)(2,1)S(1)} %get-tuple-element.7), channel_id=1, source_target_pairs={{0,32},{32,64},{64,96},{1,33},{33,65},{65,97},{2,34},{34,66},{66,9... | collective-permute-start | bytes 196616 | tf_op jit(solution)/shard_map/ppermute | solution.py:290
  13.4 5.0 %collective-permute-start.3 = (bf16[64,512]{1,0:T(8,128)(2,1)S(1)}, bf16[64,512]{1,0:T(8,128)(2,1)S(1)}, u32[]{:S(2)}, u32[]{:S(2)}) collective-permute-start(bf16[64,512]{1,0:T(8,128)(2,1)S(1)} %get-tuple-element.8), channel_id=1, source_target_pairs={{32,0},{64,32},{96,64},{33,1},{65,33},{97,65},{34,2},{66,34},{98,6... | collective-permute-start | bytes 196616 | tf_op jit(solution)/shard_map/ppermute | solution.py:290
  18.2 0.6 copy-start.7
  18.4 0.6 copy-start.8
  45.7 27.8 %all-to-all-start = ((bf16[32,64,256]{2,1,0:T(8,128)(2,1)}), bf16[32,64,256]{2,1,0:T(8,128)(2,1)S(1)}, u32[]{:S(2)}, u32[]{:S(2)}) async-start(bf16[32,64,256]{2,1,0:T(8,128)(2,1)} %get-tuple-element.11), calls=%async_computation | async-start | bytes 2097152 | tf_op jit(solution)/shard_map/all_to_all | solution.py:398

commit v5 on v4

--- a/solution.py
+++ b/solution.py
@@ -66,13 +66,12 @@
     dyn_any, tend_ref, send_ref,
     src, vsrc_ref, left_ref, right_ref, cw_ref, ext, feats, f_ref, dyn_ref, buf0, buf1, w1h, w2h, w3h,
     w1_ref, w2_ref, w3_ref, w4_ref, b1_ref, b2_ref, b3_ref, b4_ref,
-    tend_buf, send_buf, s_sems, f_sems, dyn_sems, first_sems, w_sems, tend_sems, send_sems,
+    tend_buf, send_buf, table, s_sems, f_sems, dyn_sems, first_sems, w_sems, tend_sems, send_sems,
 ):
     rows, chans, cols = f_ref.shape
     cells = rows * cols
     owners, _, cap = send_ref.shape
     slots = tend_ref.shape[0]
-    groups = slots // GROUP
     wide = cols + LANES
     chunks = rows // CHUNK
 
@@ -125,6 +124,7 @@
         f_load(k).start()
     for load in loads:
         load.start()
+    send_buf[...] = jnp.zeros(send_buf.shape, BF)
     for load in firsts:
         load.wait()
     left, right = halo_columns(left_ref, right_ref, chans)
@@ -177,26 +177,42 @@
     w2h[...] = w2_ref[...] * BF(0.5)
     w3h[...] = w3_ref[...] * BF(0.5)
 
+    each = GROUP // cap
+    step = 2 * each
+    split = owners - step
+
+    def list_owners(first, stop, begin):
+        def scan(o, n):
+            table[n] = o
+            return n + (src[0, o * cap] < cells).astype(jnp.int32)
+
+        end = lax.fori_loop(first, stop, scan, begin)
+        last = table[jnp.maximum(end - 1, 0)]
+        for extra in range(step):
+            table[end + extra] = last
+        return begin + (end - begin + step - 1) // step * step
+
+    middle = list_owners(0, split, jnp.int32(0))
+    finish = list_owners(split, owners, middle)
+
     def fetch(g, buf, start, stop):
-        base = jnp.minimum(g, groups - 1) * GROUP
+        entry = jnp.minimum(g * each, jnp.maximum(finish - each, 0))
         for r in range(start, stop, 8):
-            rows8 = feats[pl.ds(src[0, base + r], 8, stride=0), :]
+            base = table[entry + r // cap] * cap + r % cap
+            rows8 = feats[pl.ds(src[0, base], 8, stride=0), :]
             for k in range(1, 8):
-                rows8 = jnp.where(sub == k, feats[pl.ds(src[0, base + r + k], 8, stride=0), :], rows8)
+                rows8 = jnp.where(sub == k, feats[pl.ds(src[0, base + k], 8, stride=0), :], rows8)
             buf[r : r + 8, :] = rows8
 
     sub = lax.broadcasted_iota(jnp.int32, (8, LANES), 0)
     ones = jnp.ones((GROUP, LANES), BF)
 
-    each = GROUP // cap
-
-    pairs = groups // 2
-    stages = ((0, pairs - 1), (pairs - 1, pairs))
+    stages = ((0, split, 0, middle // step), (split, owners, middle // step, finish // step))
 
     def outward(n):
-        start, stop = stages[n]
-        rows_part = pl.ds(start * 2 * GROUP, (stop - start) * 2 * GROUP)
-        owner_part = pl.ds(start * 2 * each, (stop - start) * 2 * each)
+        start, stop = stages[n][:2]
+        rows_part = pl.ds(start * cap, (stop - start) * cap)
+        owner_part = pl.ds(start, stop - start)
         return (
             pltpu.make_async_copy(tend_buf.at[rows_part], tend_ref.at[rows_part], tend_sems.at[n]),
             pltpu.make_async_copy(send_buf.at[owner_part], send_ref.at[owner_part], send_sems.at[n]),
@@ -214,12 +230,12 @@
         fetch(g + 1, following, 3 * part, GROUP)
         out = jnp.dot(h, w4_ref[...], preferred_element_type=F32) + b4_ref[...]
         flip = out.T[chans:]
-        tend_buf[pl.ds(pl.multiple_of(g * GROUP, GROUP), GROUP), :] = out.astype(BF)
         for j in range(each):
-            at = pl.multiple_of((g * each + j) * cap, LANES)
-            filled = vsrc_ref[:, pl.ds(at, cap)] < cells
-            diag = jnp.where(filled, flip[:, j * cap : (j + 1) * cap], 0.0)
-            send_buf[g * each + j] = diag.astype(BF)
+            o = table[g * each + j]
+            rows_part = pl.ds(pl.multiple_of(o * cap, LANES), cap)
+            tend_buf[rows_part, :] = out[j * cap : (j + 1) * cap].astype(BF)
+            filled = vsrc_ref[:, rows_part] < cells
+            send_buf[o] = jnp.where(filled, flip[:, j * cap : (j + 1) * cap], 0.0).astype(BF)
 
     fetch(0, buf0, 0, GROUP)
 
@@ -228,7 +244,7 @@
         net(2 * i + 1, buf1, buf0)
         return carry
 
-    for n, (start, stop) in enumerate(stages):
+    for n, (_, _, start, stop) in enumerate(stages):
         lax.fori_loop(start, stop, pair, 0)
         for copy in outward(n):
             copy.start()
@@ -379,6 +395,7 @@
             pltpu.VMEM((1, 2 * chans), F32),
             pltpu.VMEM((slots, 2 * chans), BF),
             pltpu.VMEM((owners, chans, cap), BF),
+            pltpu.SMEM((2 * owners,), jnp.int32),
             pltpu.SemaphoreType.DMA((chunks,)),
             pltpu.SemaphoreType.DMA((chunks,)),
             pltpu.SemaphoreType.DMA((chunks,)),

time: 76 us -> 75.2 us (0.989); the launches traced: 74.7 us -> 75.6 us
  starting transfers between devices: 18.4 us -> 25.7 us
  Pallas kernels: 41.6 us -> 35.1 us
    all_to_all x1, starting transfers between devices: 10.8 us -> 18.1 us  [body(): got = lax.all_to_all(send, 'lon', split_axis=0, concat_axis=0, tiled=True)]
    pallas_call x1, Pallas kernels: 26.6 us -> 20.1 us  [body(): pl.pallas_call(columns_kernel, out_shape=(jax.ShapeDtypeStruct(tile_all,...]
where the time goes in v5:
time: 75.2 us; the launch traced here: 75.6 us
  Pallas kernels  35.1 us (47%)
  starting transfers between devices  25.7 us (34%)
  waiting for transfers between devices  8.36 us (11%)
  local copies, waits for them, and re-layouts  5.65 us (8%)
    pallas_call x1, Pallas kernels, body(): pl.pallas_call(columns_kernel, out_shape=(jax.ShapeDtypeStruct(tile_all,...  20.1 us
    all_to_all x1, starting transfers between devices, body(): got = lax.all_to_all(send, 'lon', split_axis=0, concat_axis=0, tiled=True)  18.1 us
    pallas_call x1, Pallas kernels, body(): pl.pallas_call(place_kernel, out_shape=jax.ShapeDtypeStruct((chans, rows,...  13 us
    ppermute x4, starting transfers between devices, shift(): return lax.ppermute(block, axis, pairs)  7.62 us
    unnamed x20, local copies, waits for them, and re-layouts  4.69 us
    ppermute x4, waiting for transfers between devices, shift(): return lax.ppermute(block, axis, pairs)  4.4 us
    all_to_all x1, waiting for transfers between devices, body(): got = lax.all_to_all(send, 'lon', split_axis=0, concat_axis=0, tiled=True)  3.96 us
  transfers between devices with their start and end apart: 5, of which 4 were waited for; matrix products, arithmetic and copies ran while one was open for 4% of the time, Pallas kernels for 17%

profile of v5, /device:TPU:9, one launch (start us, length us, event | category | flops | bytes accessed | tf_op | source)
XLA Modules:
  0.0 75.6 jit_solution(12355260178351062618)
XLA Ops:
  0.6 0.0 copy-start
  0.6 1.4 %copy-done = bf16[64,32,384]{2,1,0:T(8,128)(2,1)S(1)} copy-done((bf16[64,32,384]{2,1,0:T(8,128)(2,1)S(1)}, bf16[64,32,384]{2,1,0:T(8,128)(2,1)}, u32[]{:S(2)}) %copy-start) | copy-done | bytes 1572888
  2.0 0.0 copy-start.1
  2.0 0.5 edges.1
  2.5 0.7 collective-permute-start.1
  3.3 1.6 %collective-permute-start = (bf16[32,128]{1,0:T(8,128)(2,1)S(1)}, bf16[32,128]{1,0:T(8,128)(2,1)S(1)}, u32[]{:S(2)}, u32[]{:S(2)}) collective-permute-start(bf16[32,128]{1,0:T(8,128)(2,1)S(1)} %edges.1), channel_id=1, source_target_pairs={{0,1},{1,2},{2,3},{3,4},{4,5},{5,6},{6,7},{7,8},{8,9},{9,10},{10,1... | collective-permute-start | bytes 24584 | tf_op jit(solution)/shard_map/ppermute | solution.py:306
  4.9 0.0 copy-done.1
  4.9 0.6 copy.26
  5.5 0.0 copy-start.2
  5.5 0.7 collective-permute-done.1.right_ref.right_any
  6.1 0.0 copy-start.3
  6.2 3.5 %collective-permute-done.left_ref.left_any = bf16[32,128]{1,0:T(8,128)(2,1)S(1)} collective-permute-done((bf16[32,128]{1,0:T(8,128)(2,1)S(1)}, bf16[32,128]{1,0:T(8,128)(2,1)S(1)}, u32[]{:S(2)}, u32[]{:S(2)}) %collective-permute-start) | collective-permute-done | bytes 8224 | tf_op jit(solution)/shard_map/ppermute | solution.py:306
  9.6 0.0 copy-start.4
  9.6 0.0 copy-start.6
  9.6 0.0 copy-start.5
  9.6 0.2 rows.1
  9.8 0.0 copy-done.2
  9.8 0.0 copy-done.3
  9.8 0.4 copy-done.4
  10.2 3.2 %collective-permute-start.2 = (bf16[64,512]{1,0:T(8,128)(2,1)S(1)}, bf16[64,512]{1,0:T(8,128)(2,1)S(1)}, u32[]{:S(2)}, u32[]{:S(2)}) collective-permute-start(bf16[64,512]{1,0:T(8,128)(2,1)S(1)} %get-tuple-element.7), channel_id=1, source_target_pairs={{0,32},{32,64},{64,96},{1,33},{33,65},{65,97},{2,34},{34,66},{66,9... | collective-permute-start | bytes 196616 | tf_op jit(solution)/shard_map/ppermute | solution.py:306
  13.4 2.1 %collective-permute-start.3 = (bf16[64,512]{1,0:T(8,128)(2,1)S(1)}, bf16[64,512]{1,0:T(8,128)(2,1)S(1)}, u32[]{:S(2)}, u32[]{:S(2)}) collective-permute-start(bf16[64,512]{1,0:T(8,128)(2,1)S(1)} %get-tuple-element.8), channel_id=1, source_target_pairs={{32,0},{64,32},{96,64},{33,1},{65,33},{97,65},{34,2},{66,34},{98,6... | collective-permute-start | bytes 196616 | tf_op jit(solution)/shard_map/ppermute | solution.py:306
  15.5 0.0 copy-done.6
  15.5 0.1 copy.27
  15.7 0.8 %reshape.30.cw_any = bf16[192,192]{1,0:T(8,128)(2,1)} reshape(bf16[3,64,3,64]{3,2,1,0:T(4,128)(2,1)S(1)} %bitcast.23) | data formatting | bytes 147456 | tf_op jit(solution)/shard_map/reshape | solution.py:343
  16.5 0.0 copy-done.5
  16.5 1.7 %copy.25 = bf16[64,32,384]{2,0,1:T(8,128)(2,1)} copy(bf16[64,32,384]{2,1,0:T(8,128)(2,1)S(1)} %copy-done.5) | data formatting | bytes 3145728 | tf_op args[1]
  18.2 0.0 collective-permute-done.2.top_any
  18.2 0.0 copy-start.7
  18.2 0.2 collective-permute-done.3.bot_any
  18.4 0.0 copy-start.8
  18.4 0.4 copy-done.7
  18.8 0.2 copy-done.8
  19.1 20.1 %columns.1 = (bf16[32,64,384]{2,1,0:T(8,128)(2,1)}, bf16[8192,128]{1,0:T(8,128)(2,1)}, bf16[32,64,256]{2,1,0:T(8,128)(2,1)}) custom-call(s32[1,8192]{1,0:T(1,128)} %bitcast.25, bf16[32,64,384]{2,1,0:T(8,128)(2,1)} %bitcast.20, bf16[32,128]{1,0:T(8,128)(2,1)} %copy-done.4, bf16[32,128]{1,0:T(8,128)(2,1)} %copy-done.3, bf16[64,512]{1,0:T(8,128)(2,1)} %copy-done.7, ...), custom_call_target="tpu_custom_call" | custom-call | flops 10000000000 | bytes 8000000 | tf_op jit(solution)/shard_map/columns/pallas_call | solution.py:364
  39.2 18.1 %all-to-all-start = ((bf16[32,64,256]{2,1,0:T(8,128)(2,1)}), bf16[32,64,256]{2,1,0:T(8,128)(2,1)S(1)}, u32[]{:S(2)}, u32[]{:S(2)}) async-start(bf16[32,64,256]{2,1,0:T(8,128)(2,1)} %get-tuple-element.11), calls=%async_computation | async-start | bytes 2097152 | tf_op jit(solution)/shard_map/all_to_all | solution.py:415
  57.4 13.0 %place.1 = bf16[64,32,384]{2,1,0:T(8,128)(2,1)} custom-call(s32[1,8192]{1,0:T(1,128)} %bitcast.26, bf16[32,64,384]{2,1,0:T(8,128)(2,1)} %get-tuple-element.9.dyn_any, bf16[8192,128]{1,0:T(8,128)(2,1)} %get-tuple-element.10.tend_any), custom_call_target="tpu_custom_call" | custom-call | flops 5000000000 | bytes 8000000 | tf_op jit(solution)/shard_map/place/pallas_call | solution.py:416
  70.4 4.0 %all-to-all-done.got_ref = bf16[32,64,256]{2,1,0:T(8,128)(2,1)S(1)} async-done(((bf16[32,64,256]{2,1,0:T(8,128)(2,1)}), bf16[32,64,256]{2,1,0:T(8,128)(2,1)S(1)}, u32[]{:S(2)}, u32[]{:S(2)}) %all-to-all-start) | async-done | bytes 1048608 | tf_op jit(solution)/shard_map/all_to_all | solution.py:415
  74.4 1.2 %owned.1 = bf16[64,32,256]{2,1,0:T(8,128)(2,1)} custom-call(bf16[32,64,256]{2,1,0:T(8,128)(2,1)S(1)} %all-to-all-done.got_ref), custom_call_target="tpu_custom_call" | custom-call | tf_op jit(solution)/shard_map/owned/pallas_call | solution.py:433
Async XLA Ops:
  0.6 1.4 %copy-start = (bf16[64,32,384]{2,1,0:T(8,128)(2,1)S(1)}, bf16[64,32,384]{2,1,0:T(8,128)(2,1)}, u32[]{:S(2)}) copy-start(bf16[64,32,384]{2,1,0:T(8,128)(2,1)} %high_ref.1) | copy-start | bytes 4718596
  2.0 2.9 %copy-start.1 = (bf16[64,32,384]{2,1,0:T(8,128)(2,1)S(1)}, bf16[64,32,384]{2,1,0:T(8,128)(2,1)}, u32[]{:S(2)}) copy-start(bf16[64,32,384]{2,1,0:T(8,128)(2,1)} %high_ref.1) | copy-start | bytes 4718596
  2.5 3.6 %collective-permute-start.1 = (bf16[32,128]{1,0:T(8,128)(2,1)S(1)}, bf16[32,128]{1,0:T(8,128)(2,1)S(1)}, u32[]{:S(2)}, u32[]{:S(2)}) collective-permute-start(bf16[32,128]{1,0:T(8,128)(2,1)S(1)} %edges.1), channel_id=1, source_target_pairs={{0,31},{1,0},{2,1},{3,2},{4,3},{5,4},{6,5},{7,6},{8,7},{9,8},{10,9... | collective-permute-start | bytes 24584 | tf_op jit(solution)/shard_map/ppermute | solution.py:306
  3.3 6.3 %collective-permute-start = (bf16[32,128]{1,0:T(8,128)(2,1)S(1)}, bf16[32,128]{1,0:T(8,128)(2,1)S(1)}, u32[]{:S(2)}, u32[]{:S(2)}) collective-permute-start(bf16[32,128]{1,0:T(8,128)(2,1)S(1)} %edges.1), channel_id=1, source_target_pairs={{0,1},{1,2},{2,3},{3,4},{4,5},{5,6},{6,7},{7,8},{8,9},{9,10},{10,1... | collective-permute-start | bytes 24584 | tf_op jit(solution)/shard_map/ppermute | solution.py:306
  5.5 4.4 %copy-start.2 = (bf16[64,32,384]{2,0,1:T(8,128)(2,1)}, bf16[64,32,384]{2,0,1:T(8,128)(2,1)S(1)}, u32[]{:S(2)}) copy-start(bf16[64,32,384]{2,0,1:T(8,128)(2,1)S(1)} %copy.26) | copy-start | bytes 4718596
  6.1 3.7 %copy-start.3 = (bf16[32,128]{1,0:T(8,128)(2,1)}, bf16[32,128]{1,0:T(8,128)(2,1)S(1)}, u32[]{:S(2)}) copy-start(bf16[32,128]{1,0:T(8,128)(2,1)S(1)} %collective-permute-done.1.right_ref.right_any) | copy-start | bytes 24580
  9.6 0.6 copy-start.4
  9.6 5.9 %copy-start.6 = (bf16[9,64,64]{2,1,0:T(8,128)(2,1)S(1)}, bf16[9,64,64]{2,1,0:T(8,128)(2,1)}, u32[]{:S(2)}) copy-start(bf16[9,64,64]{2,1,0:T(8,128)(2,1)} %param.17) | copy-start | bytes 221188
  9.6 6.9 %copy-start.5 = (bf16[64,32,384]{2,1,0:T(8,128)(2,1)S(1)}, bf16[64,32,384]{2,1,0:T(8,128)(2,1)}, u32[]{:S(2)}) copy-start(bf16[64,32,384]{2,1,0:T(8,128)(2,1)} %param.16) | copy-start | bytes 4718596
  10.2 8.0 %collective-permute-start.2 = (bf16[64,512]{1,0:T(8,128)(2,1)S(1)}, bf16[64,512]{1,0:T(8,128)(2,1)S(1)}, u32[]{:S(2)}, u32[]{:S(2)}) collective-permute-start(bf16[64,512]{1,0:T(8,128)(2,1)S(1)} %get-tuple-element.7), channel_id=1, source_target_pairs={{0,32},{32,64},{64,96},{1,33},{33,65},{65,97},{2,34},{34,66},{66,9... | collective-permute-start | bytes 196616 | tf_op jit(solution)/shard_map/ppermute | solution.py:306
  13.4 5.0 %collective-permute-start.3 = (bf16[64,512]{1,0:T(8,128)(2,1)S(1)}, bf16[64,512]{1,0:T(8,128)(2,1)S(1)}, u32[]{:S(2)}, u32[]{:S(2)}) collective-permute-start(bf16[64,512]{1,0:T(8,128)(2,1)S(1)} %get-tuple-element.8), channel_id=1, source_target_pairs={{32,0},{64,32},{96,64},{33,1},{65,33},{97,65},{34,2},{66,34},{98,6... | collective-permute-start | bytes 196616 | tf_op jit(solution)/shard_map/ppermute | solution.py:306
  18.2 0.6 copy-start.7
  18.4 0.6 copy-start.8
  39.2 35.1 %all-to-all-start = ((bf16[32,64,256]{2,1,0:T(8,128)(2,1)}), bf16[32,64,256]{2,1,0:T(8,128)(2,1)S(1)}, u32[]{:S(2)}, u32[]{:S(2)}) async-start(bf16[32,64,256]{2,1,0:T(8,128)(2,1)} %get-tuple-element.11), calls=%async_computation | async-start | bytes 2097152 | tf_op jit(solution)/shard_map/all_to_all | solution.py:415

commit v6 on v5

--- a/solution.py
+++ b/solution.py
@@ -9,7 +9,7 @@
 K1 = K0 * 0.044715
 LANES = 128
 GROUP = 512
-CHUNK = 8
+CHUNK = 16
 PITCH = 33
 BF = jnp.bfloat16
 F32 = jnp.float32
@@ -163,20 +163,6 @@
 
     for load in loads:
         load.wait()
-    hid = w2h.shape[0]
-    half = b1_ref[...] * 0.5
-    high = half.astype(BF)
-    rest = half - high.astype(F32)
-    mid = rest.astype(BF)
-    low = (rest - mid.astype(F32)).astype(BF)
-    row = lax.broadcasted_iota(jnp.int32, (LANES, hid), 0)
-    w1h[:LANES] = w1_ref[...] * BF(0.5)
-    w1h[LANES:] = jnp.where(
-        row == 0, high.astype(F32), jnp.where(row == 1, mid.astype(F32), jnp.where(row == 2, low.astype(F32), 0.0))
-    ).astype(BF)
-    w2h[...] = w2_ref[...] * BF(0.5)
-    w3h[...] = w3_ref[...] * BF(0.5)
-
     each = GROUP // cap
     step = 2 * each
     split = owners - step
@@ -236,6 +222,20 @@
             tend_buf[rows_part, :] = out[j * cap : (j + 1) * cap].astype(BF)
             filled = vsrc_ref[:, rows_part] < cells
             send_buf[o] = jnp.where(filled, flip[:, j * cap : (j + 1) * cap], 0.0).astype(BF)
+
+    hid = w2h.shape[0]
+    half = b1_ref[...] * 0.5
+    high = half.astype(BF)
+    rest = half - high.astype(F32)
+    mid = rest.astype(BF)
+    low = (rest - mid.astype(F32)).astype(BF)
+    row = lax.broadcasted_iota(jnp.int32, (LANES, hid), 0)
+    w1h[:LANES] = w1_ref[...] * BF(0.5)
+    w1h[LANES:] = jnp.where(
+        row == 0, high.astype(F32), jnp.where(row == 1, mid.astype(F32), jnp.where(row == 2, low.astype(F32), 0.0))
+    ).astype(BF)
+    w2h[...] = w2_ref[...] * BF(0.5)
+    w3h[...] = w3_ref[...] * BF(0.5)
 
     fetch(0, buf0, 0, GROUP)
 

time: 75.2 us -> 75.9 us (level); the launches traced: 75.6 us -> 75.5 us
  no operation moved by 1% of the time
where the time goes in v6:
time: 75.9 us; the launch traced here: 75.5 us
  Pallas kernels  35 us (46%)
  starting transfers between devices  25.7 us (34%)
  waiting for transfers between devices  8.36 us (11%)
  local copies, waits for them, and re-layouts  5.65 us (7%)
    pallas_call x1, Pallas kernels, body(): pl.pallas_call(columns_kernel, out_shape=(jax.ShapeDtypeStruct(tile_all,...  20 us
    all_to_all x1, starting transfers between devices, body(): got = lax.all_to_all(send, 'lon', split_axis=0, concat_axis=0, tiled=True)  18.1 us
    pallas_call x1, Pallas kernels, body(): pl.pallas_call(place_kernel, out_shape=jax.ShapeDtypeStruct((chans, rows,...  13 us
    ppermute x4, starting transfers between devices, shift(): return lax.ppermute(block, axis, pairs)  7.62 us
    unnamed x20, local copies, waits for them, and re-layouts  4.69 us
    ppermute x4, waiting for transfers between devices, shift(): return lax.ppermute(block, axis, pairs)  4.4 us
    all_to_all x1, waiting for transfers between devices, body(): got = lax.all_to_all(send, 'lon', split_axis=0, concat_axis=0, tiled=True)  3.96 us
  transfers between devices with their start and end apart: 5, of which 4 were waited for; matrix products, arithmetic and copies ran while one was open for 4% of the time, Pallas kernels for 17%

profile of v6, /device:TPU:9, one launch (start us, length us, event | category | flops | bytes accessed | tf_op | source)
XLA Modules:
  0.0 75.5 jit_solution(5095626027109151479)
XLA Ops:
  0.6 0.0 copy-start
  0.6 1.4 %copy-done = bf16[64,32,384]{2,1,0:T(8,128)(2,1)S(1)} copy-done((bf16[64,32,384]{2,1,0:T(8,128)(2,1)S(1)}, bf16[64,32,384]{2,1,0:T(8,128)(2,1)}, u32[]{:S(2)}) %copy-start) | copy-done | bytes 1572888
  2.0 0.0 copy-start.1
  2.0 0.5 edges.1
  2.5 0.7 collective-permute-start.1
  3.3 1.6 %collective-permute-start = (bf16[32,128]{1,0:T(8,128)(2,1)S(1)}, bf16[32,128]{1,0:T(8,128)(2,1)S(1)}, u32[]{:S(2)}, u32[]{:S(2)}) collective-permute-start(bf16[32,128]{1,0:T(8,128)(2,1)S(1)} %edges.1), channel_id=1, source_target_pairs={{0,1},{1,2},{2,3},{3,4},{4,5},{5,6},{6,7},{7,8},{8,9},{9,10},{10,1... | collective-permute-start | bytes 24584 | tf_op jit(solution)/shard_map/ppermute | solution.py:306
  4.9 0.0 copy-done.1
  4.9 0.6 copy.26
  5.5 0.0 copy-start.2
  5.5 0.7 collective-permute-done.1.right_ref.right_any
  6.1 0.0 copy-start.3
  6.2 3.5 %collective-permute-done.left_ref.left_any = bf16[32,128]{1,0:T(8,128)(2,1)S(1)} collective-permute-done((bf16[32,128]{1,0:T(8,128)(2,1)S(1)}, bf16[32,128]{1,0:T(8,128)(2,1)S(1)}, u32[]{:S(2)}, u32[]{:S(2)}) %collective-permute-start) | collective-permute-done | bytes 8224 | tf_op jit(solution)/shard_map/ppermute | solution.py:306
  9.6 0.0 copy-start.4
  9.6 0.0 copy-start.6
  9.6 0.0 copy-start.5
  9.6 0.2 rows.1
  9.8 0.0 copy-done.2
  9.8 0.0 copy-done.3
  9.8 0.4 copy-done.4
  10.2 3.2 %collective-permute-start.2 = (bf16[64,512]{1,0:T(8,128)(2,1)S(1)}, bf16[64,512]{1,0:T(8,128)(2,1)S(1)}, u32[]{:S(2)}, u32[]{:S(2)}) collective-permute-start(bf16[64,512]{1,0:T(8,128)(2,1)S(1)} %get-tuple-element.7), channel_id=1, source_target_pairs={{0,32},{32,64},{64,96},{1,33},{33,65},{65,97},{2,34},{34,66},{66,9... | collective-permute-start | bytes 196616 | tf_op jit(solution)/shard_map/ppermute | solution.py:306
  13.4 2.1 %collective-permute-start.3 = (bf16[64,512]{1,0:T(8,128)(2,1)S(1)}, bf16[64,512]{1,0:T(8,128)(2,1)S(1)}, u32[]{:S(2)}, u32[]{:S(2)}) collective-permute-start(bf16[64,512]{1,0:T(8,128)(2,1)S(1)} %get-tuple-element.8), channel_id=1, source_target_pairs={{32,0},{64,32},{96,64},{33,1},{65,33},{97,65},{34,2},{66,34},{98,6... | collective-permute-start | bytes 196616 | tf_op jit(solution)/shard_map/ppermute | solution.py:306
  15.5 0.0 copy-done.6
  15.5 0.1 copy.27
  15.7 0.8 %reshape.30.cw_any = bf16[192,192]{1,0:T(8,128)(2,1)} reshape(bf16[3,64,3,64]{3,2,1,0:T(4,128)(2,1)S(1)} %bitcast.23) | data formatting | bytes 147456 | tf_op jit(solution)/shard_map/reshape | solution.py:343
  16.5 0.0 copy-done.5
  16.5 1.7 %copy.25 = bf16[64,32,384]{2,0,1:T(8,128)(2,1)} copy(bf16[64,32,384]{2,1,0:T(8,128)(2,1)S(1)} %copy-done.5) | data formatting | bytes 3145728 | tf_op args[1]
  18.2 0.0 collective-permute-done.2.top_any
  18.2 0.0 copy-start.7
  18.2 0.2 collective-permute-done.3.bot_any
  18.4 0.0 copy-start.8
  18.4 0.4 copy-done.7
  18.8 0.2 copy-done.8
  19.1 20.0 %columns.1 = (bf16[32,64,384]{2,1,0:T(8,128)(2,1)}, bf16[8192,128]{1,0:T(8,128)(2,1)}, bf16[32,64,256]{2,1,0:T(8,128)(2,1)}) custom-call(s32[1,8192]{1,0:T(1,128)} %bitcast.25, bf16[32,64,384]{2,1,0:T(8,128)(2,1)} %bitcast.20, bf16[32,128]{1,0:T(8,128)(2,1)} %copy-done.4, bf16[32,128]{1,0:T(8,128)(2,1)} %copy-done.3, bf16[64,512]{1,0:T(8,128)(2,1)} %copy-done.7, ...), custom_call_target="tpu_custom_call" | custom-call | flops 10000000000 | bytes 8000000 | tf_op jit(solution)/shard_map/columns/pallas_call | solution.py:364
  39.1 18.1 %all-to-all-start = ((bf16[32,64,256]{2,1,0:T(8,128)(2,1)}), bf16[32,64,256]{2,1,0:T(8,128)(2,1)S(1)}, u32[]{:S(2)}, u32[]{:S(2)}) async-start(bf16[32,64,256]{2,1,0:T(8,128)(2,1)} %get-tuple-element.11), calls=%async_computation | async-start | bytes 2097152 | tf_op jit(solution)/shard_map/all_to_all | solution.py:415
  57.2 13.0 %place.1 = bf16[64,32,384]{2,1,0:T(8,128)(2,1)} custom-call(s32[1,8192]{1,0:T(1,128)} %bitcast.26, bf16[32,64,384]{2,1,0:T(8,128)(2,1)} %get-tuple-element.9.dyn_any, bf16[8192,128]{1,0:T(8,128)(2,1)} %get-tuple-element.10.tend_any), custom_call_target="tpu_custom_call" | custom-call | flops 5000000000 | bytes 8000000 | tf_op jit(solution)/shard_map/place/pallas_call | solution.py:416
  70.3 4.0 %all-to-all-done.got_ref = bf16[32,64,256]{2,1,0:T(8,128)(2,1)S(1)} async-done(((bf16[32,64,256]{2,1,0:T(8,128)(2,1)}), bf16[32,64,256]{2,1,0:T(8,128)(2,1)S(1)}, u32[]{:S(2)}, u32[]{:S(2)}) %all-to-all-start) | async-done | bytes 1048608 | tf_op jit(solution)/shard_map/all_to_all | solution.py:415
  74.2 1.2 %owned.1 = bf16[64,32,256]{2,1,0:T(8,128)(2,1)} custom-call(bf16[32,64,256]{2,1,0:T(8,128)(2,1)S(1)} %all-to-all-done.got_ref), custom_call_target="tpu_custom_call" | custom-call | tf_op jit(solution)/shard_map/owned/pallas_call | solution.py:433
Async XLA Ops:
  0.6 1.4 %copy-start = (bf16[64,32,384]{2,1,0:T(8,128)(2,1)S(1)}, bf16[64,32,384]{2,1,0:T(8,128)(2,1)}, u32[]{:S(2)}) copy-start(bf16[64,32,384]{2,1,0:T(8,128)(2,1)} %high_ref.1) | copy-start | bytes 4718596
  2.0 2.9 %copy-start.1 = (bf16[64,32,384]{2,1,0:T(8,128)(2,1)S(1)}, bf16[64,32,384]{2,1,0:T(8,128)(2,1)}, u32[]{:S(2)}) copy-start(bf16[64,32,384]{2,1,0:T(8,128)(2,1)} %high_ref.1) | copy-start | bytes 4718596
  2.5 3.6 %collective-permute-start.1 = (bf16[32,128]{1,0:T(8,128)(2,1)S(1)}, bf16[32,128]{1,0:T(8,128)(2,1)S(1)}, u32[]{:S(2)}, u32[]{:S(2)}) collective-permute-start(bf16[32,128]{1,0:T(8,128)(2,1)S(1)} %edges.1), channel_id=1, source_target_pairs={{0,31},{1,0},{2,1},{3,2},{4,3},{5,4},{6,5},{7,6},{8,7},{9,8},{10,9... | collective-permute-start | bytes 24584 | tf_op jit(solution)/shard_map/ppermute | solution.py:306
  3.3 6.3 %collective-permute-start = (bf16[32,128]{1,0:T(8,128)(2,1)S(1)}, bf16[32,128]{1,0:T(8,128)(2,1)S(1)}, u32[]{:S(2)}, u32[]{:S(2)}) collective-permute-start(bf16[32,128]{1,0:T(8,128)(2,1)S(1)} %edges.1), channel_id=1, source_target_pairs={{0,1},{1,2},{2,3},{3,4},{4,5},{5,6},{6,7},{7,8},{8,9},{9,10},{10,1... | collective-permute-start | bytes 24584 | tf_op jit(solution)/shard_map/ppermute | solution.py:306
  5.5 4.4 %copy-start.2 = (bf16[64,32,384]{2,0,1:T(8,128)(2,1)}, bf16[64,32,384]{2,0,1:T(8,128)(2,1)S(1)}, u32[]{:S(2)}) copy-start(bf16[64,32,384]{2,0,1:T(8,128)(2,1)S(1)} %copy.26) | copy-start | bytes 4718596
  6.1 3.7 %copy-start.3 = (bf16[32,128]{1,0:T(8,128)(2,1)}, bf16[32,128]{1,0:T(8,128)(2,1)S(1)}, u32[]{:S(2)}) copy-start(bf16[32,128]{1,0:T(8,128)(2,1)S(1)} %collective-permute-done.1.right_ref.right_any) | copy-start | bytes 24580
  9.6 0.6 copy-start.4
  9.6 5.9 %copy-start.6 = (bf16[9,64,64]{2,1,0:T(8,128)(2,1)S(1)}, bf16[9,64,64]{2,1,0:T(8,128)(2,1)}, u32[]{:S(2)}) copy-start(bf16[9,64,64]{2,1,0:T(8,128)(2,1)} %param.17) | copy-start | bytes 221188
  9.6 6.9 %copy-start.5 = (bf16[64,32,384]{2,1,0:T(8,128)(2,1)S(1)}, bf16[64,32,384]{2,1,0:T(8,128)(2,1)}, u32[]{:S(2)}) copy-start(bf16[64,32,384]{2,1,0:T(8,128)(2,1)} %param.16) | copy-start | bytes 4718596
  10.2 8.0 %collective-permute-start.2 = (bf16[64,512]{1,0:T(8,128)(2,1)S(1)}, bf16[64,512]{1,0:T(8,128)(2,1)S(1)}, u32[]{:S(2)}, u32[]{:S(2)}) collective-permute-start(bf16[64,512]{1,0:T(8,128)(2,1)S(1)} %get-tuple-element.7), channel_id=1, source_target_pairs={{0,32},{32,64},{64,96},{1,33},{33,65},{65,97},{2,34},{34,66},{66,9... | collective-permute-start | bytes 196616 | tf_op jit(solution)/shard_map/ppermute | solution.py:306
  13.4 5.0 %collective-permute-start.3 = (bf16[64,512]{1,0:T(8,128)(2,1)S(1)}, bf16[64,512]{1,0:T(8,128)(2,1)S(1)}, u32[]{:S(2)}, u32[]{:S(2)}) collective-permute-start(bf16[64,512]{1,0:T(8,128)(2,1)S(1)} %get-tuple-element.8), channel_id=1, source_target_pairs={{32,0},{64,32},{96,64},{33,1},{65,33},{97,65},{34,2},{66,34},{98,6... | collective-permute-start | bytes 196616 | tf_op jit(solution)/shard_map/ppermute | solution.py:306
  18.2 0.6 copy-start.7
  18.4 0.6 copy-start.8
  39.1 35.1 %all-to-all-start = ((bf16[32,64,256]{2,1,0:T(8,128)(2,1)}), bf16[32,64,256]{2,1,0:T(8,128)(2,1)S(1)}, u32[]{:S(2)}, u32[]{:S(2)}) async-start(bf16[32,64,256]{2,1,0:T(8,128)(2,1)} %get-tuple-element.11), calls=%async_computation | async-start | bytes 2097152 | tf_op jit(solution)/shard_map/all_to_all | solution.py:415
